TPU v7x, 32 devices: a whole 2x2x4 slice. The times are simulated.
32 devices in a mesh: depth: 4 (over x, core), tile: 8 (over z, y).
Axes of the slice: x: 2, y: 2, z: 4, core: 2. Of those that a mesh axis runs over, the one named last changes fastest.
Arguments:
- volume: bfloat16 [256, 128, 1024], P('depth', 'tile'), may hold values from -6 to 6
- knot_pos: int32 [16], replicated, may hold values from 0 to 255, as said below
- knot_color: int32 [4, 16], replicated, may hold values from 0 to 255
Outputs:
- image: float32 [4, 128, 1024], P(None, 'tile', 'depth')
Inputs may be any that keep to these rules, and one draw needn't show every extreme that they name: `knot_pos`: strictly increasing with neighbouring breakpoints 9 or more apart; the first is 0 and the last 255.
All inputs are finite; a program needn't handle non-finite values.
Results may differ from a plain program's by a relative error of at most 0.0003.
Values may be sent and summed in bfloat16 or wider, within the bound.
A program may use at most 128 MiB of HBM per device.

v0:
```python
import jax
import jax.numpy as jnp
from jax import lax
from jax.sharding import PartitionSpec as P


def padded(block, sides, width):
    for axis, dim in sides:
        count = lax.axis_size(axis)
        forward = [(i, i + 1) for i in range(count - 1)]
        backward = [(target, source) for source, target in forward]
        low = lax.ppermute(
            lax.slice_in_dim(block, block.shape[dim] - width, None, axis=dim), axis, forward
        )
        high = lax.ppermute(lax.slice_in_dim(block, 0, width, axis=dim), axis, backward)
        block = jnp.concatenate([low, block, high], axis=dim)
    return block


def carried_in(value, axis, join, neutral):
    count, mine = (lax.axis_size(axis), lax.axis_index(axis))
    pieces = lax.all_gather(value, axis)
    subtotal = jnp.full_like(value, 0) + jnp.asarray(neutral, value.dtype)

    def hop(position, subtotal):
        longer = join(subtotal, pieces[position])
        return jnp.where(position < mine, longer, subtotal)

    return lax.fori_loop(0, count - 1, hop, subtotal)


def next_along(center):
    return jnp.pad(center[:, :, 1:], ((0, 0), (0, 0), (0, 1)))


def prior_along(center):
    return jnp.pad(center[:, :, :-1], ((0, 0), (0, 0), (1, 0)))


def smooth_block(extended):
    field = extended.astype(jnp.float32)
    center = field[1:-1, 1:-1]
    neighbours = field[2:, 1:-1] + field[:-2, 1:-1] + field[1:-1, 2:] + field[1:-1, :-2]
    neighbours = neighbours + next_along(center) + prior_along(center)
    return 0.4 * center + 0.1 * neighbours


def hat_colors(lookup, knot_pos, knot_color):
    knot_float = knot_pos.astype(jnp.float32)
    palette = knot_color.astype(jnp.float32) / 255.0
    count = knot_pos.shape[0]
    colors = [jnp.zeros_like(lookup) for c in range(3)]
    extinction = jnp.zeros_like(lookup)
    for k in range(count):
        if k == 0:
            weight = jnp.clip((knot_float[1] - lookup) / (knot_float[1] - knot_float[0]), 0.0, 1.0)
        elif k == count - 1:
            weight = jnp.clip(
                (lookup - knot_float[k - 1]) / (knot_float[k] - knot_float[k - 1]), 0.0, 1.0
            )
        else:
            rising = (lookup - knot_float[k - 1]) / (knot_float[k] - knot_float[k - 1])
            falling = (knot_float[k + 1] - lookup) / (knot_float[k + 1] - knot_float[k])
            weight = jnp.maximum(0.0, jnp.minimum(rising, falling))
        colors = [colors[c] + weight * palette[c, k] for c in range(3)]
        extinction = extinction + weight * palette[3, k]
    return (colors, extinction)


def shade_classify(smooth_ext, knot_pos, knot_color, sigma_scale):
    field = smooth_ext.astype(jnp.float32)
    center = field[1:-1, 1:-1]
    slope_z = 0.5 * (field[2:, 1:-1] - field[:-2, 1:-1])
    slope_x = 0.5 * (field[1:-1, 2:] - field[1:-1, :-2])
    slope_y = 0.5 * (next_along(center) - prior_along(center))
    facing = jnp.abs(0.6 * slope_z + 0.8 * slope_x)
    shading = 0.3 + 0.7 * facing / jnp.sqrt(
        slope_z * slope_z + slope_x * slope_x + slope_y * slope_y + 0.1
    )
    knot_float = knot_pos.astype(jnp.float32)
    lookup = jnp.clip(127.5 + 70.0 * center, knot_float[0], knot_float[-1])
    colors, extinction = hat_colors(lookup, knot_pos, knot_color)
    return (shading, colors, extinction * sigma_scale)


def composite(shading, colors, extinction):
    before = jnp.cumsum(extinction, axis=0) - extinction
    weight = shading * (1.0 - jnp.exp(-extinction)) * jnp.exp(-before)
    brick_color = jnp.stack([jnp.sum(weight * colors[c], axis=0) for c in range(3)])
    return (brick_color, jnp.sum(extinction, axis=0))


def add_terms(earlier, later):
    return earlier + later


def body(volume, knot_pos, knot_color):
    depth_count = lax.axis_size("depth")
    brick_depth, brick_rows, row_width = volume.shape
    sigma_scale = 4.0 / (brick_depth * depth_count)
    extended = padded(volume, (("depth", 0), ("tile", 1)), 1)
    smoothed = smooth_block(extended).astype(jnp.bfloat16)
    smooth_ext = padded(smoothed, (("depth", 0), ("tile", 1)), 1)
    shading, colors, extinction = shade_classify(smooth_ext, knot_pos, knot_color, sigma_scale)
    brick_color, optical_depth = composite(shading, colors, extinction)
    optical_ahead = carried_in(optical_depth, "depth", add_terms, jnp.zeros_like(optical_depth))
    attenuation = jnp.exp(-optical_ahead)
    weighted = jnp.concatenate([brick_color * attenuation[None], optical_depth[None]], axis=0)
    merged = lax.psum_scatter(weighted, "depth", scatter_dimension=2, tiled=True)
    return jnp.concatenate([merged[:3], 1.0 - jnp.exp(-merged[3:])], axis=0)


def solution(mesh):
    in_specs = (P("depth", "tile", None), P(), P())
    out_specs = P(None, "tile", "depth")
    return jax.shard_map(body, mesh=mesh, in_specs=in_specs, out_specs=out_specs, check_vma=False)
```

profile of v0, /device:TPU:21, one launch (start us, length us, event | category | flops | bytes accessed | tf_op | source)
XLA Modules:
  0.0 293.5 jit_solution(107295606107700010)
XLA Ops:
  7.3 3.7 %collective-permute-start = (bf16[1,16,1024]{2,1,0:T(8,128)(2,1)S(1)}, bf16[1,16,1024]{2,1,0:T(8,128)(2,1)S(1)}, u32[]{:S(2)}, u32[]{:S(2)}) collective-permute-start(bf16[1,16,1024]{2,1,0:T(8,128)(2,1)S(1)} %get-tuple-element.123), channel_id=1, source_target_pairs={{0,8},{8,16},{16,24},{1,9},{9,17},{17,25},{2,10},{10,18},{18,26},{... | collective-permute-start | bytes 98312 | tf_op jit(solution)/shard_map/ppermute | solution.py:12
  11.0 1.9 collective-permute-start.1
  13.6 1.8 constant_dynamic-update-slice_fusion.1
  16.7 2.1 collective-permute-start.3
  18.9 4.0 %collective-permute-start.2 = (bf16[66,1,1024]{2,1,0:T(2,128)(2,1)S(1)}, bf16[66,1,1024]{2,1,0:T(2,128)(2,1)S(1)}, u32[]{:S(2)}, u32[]{:S(2)}) collective-permute-start(bf16[66,1,1024]{2,1,0:T(2,128)(2,1)S(1)} %get-tuple-element.118), channel_id=1, source_target_pairs={{0,1},{1,2},{2,3},{3,4},{4,5},{5,6},{6,7},{8,9},{9,10},{10,11},{11... | collective-permute-start | bytes 405512 | tf_op jit(solution)/shard_map/ppermute | solution.py:12
  24.4 4.9 %collective-permute-done.3 = bf16[66,1,1024]{2,1,0:T(2,128)(2,1)S(1)} collective-permute-done((bf16[66,1,1024]{2,1,0:T(2,128)(2,1)S(1)}, bf16[66,1,1024]{2,1,0:T(2,128)(2,1)S(1)}, u32[]{:S(2)}, u32[]{:S(2)}) %collective-permute-start.3) | collective-permute-done | bytes 135200 | tf_op jit(solution)/shard_map/ppermute | solution.py:15
  29.3 2.8 collective-permute-done.2
  32.0 1.7 maximum_convert_fusion
  33.7 4.3 %fusion.12 = (f32[64,16,1023]{2,1,0:T(8,128)S(1)}, f32[64,16,1023]{2,1,0:T(8,128)}) fusion(f32[66,18,1024]{2,1,0:T(8,128)S(1)} %maximum_convert_fusion), kind=kLoop, calls=%fused_computation.56 | loop fusion | bytes 16760832 | tf_op jit(solution)/shard_map/slice | solution.py:33
  38.0 6.0 %fusion.7 = bf16[64,16,1024]{2,1,0:T(8,128)(2,1)S(1)} fusion(f32[66,18,1024]{2,1,0:T(8,128)S(1)} %maximum_convert_fusion, f32[64,16,1023]{2,1,0:T(8,128)} %get-tuple-element.115, f32[64,16,1023]{2,1,0:T(8,128)S(1)} %get-tuple-element.114), kind=kLoop, calls=%fused_computation.12 | loop fusion | flops 9437184 | bytes 31449088 | tf_op jit(solution)/shard_map/convert_element_type | solution.py:102
  44.0 2.3 collective-permute-start.5
  46.3 3.3 %collective-permute-start.4 = (bf16[1,16,1024]{2,1,0:T(8,128)(2,1)S(1)}, bf16[1,16,1024]{2,1,0:T(8,128)(2,1)S(1)}, u32[]{:S(2)}, u32[]{:S(2)}) collective-permute-start(bf16[1,16,1024]{2,1,0:T(8,128)(2,1)S(1)} %get-tuple-element.120), channel_id=1, source_target_pairs={{0,8},{8,16},{16,24},{1,9},{9,17},{17,25},{2,10},{10,18},{18,26},{... | collective-permute-start | bytes 98312 | tf_op jit(solution)/shard_map/ppermute | solution.py:12
  51.0 1.9 collective-permute-start.7
  53.0 4.4 %collective-permute-start.6 = (bf16[66,1,1024]{2,1,0:T(2,128)(2,1)S(1)}, bf16[66,1,1024]{2,1,0:T(2,128)(2,1)S(1)}, u32[]{:S(2)}, u32[]{:S(2)}) collective-permute-start(bf16[66,1,1024]{2,1,0:T(2,128)(2,1)S(1)} %get-tuple-element.116), channel_id=1, source_target_pairs={{0,1},{1,2},{2,3},{3,4},{4,5},{5,6},{6,7},{8,9},{9,10},{10,11},{11... | collective-permute-start | bytes 405512 | tf_op jit(solution)/shard_map/ppermute | solution.py:12
  77.8 1.8 maximum_convert_fusion.1
  79.6 5.4 %fusion.11 = (f32[64,16,1023]{2,1,0:T(8,128)}, f32[64,16,1023]{2,1,0:T(8,128)}) fusion(f32[66,18,1024]{2,1,0:T(8,128)S(1)} %maximum_convert_fusion.1), kind=kLoop, calls=%fused_computation.55 | loop fusion | bytes 16760832 | tf_op jit(solution)/shard_map/slice | solution.py:33
  85.0 37.9 %fusion.10 = (f32[16,1024]{1,0:T(8,128)S(1)}, f32[64,16,1024]{2,1,0:T(8,128)S(1)}) fusion(f32[]{:T(128)} %bitcast.31, f32[]{:T(128)} %bitcast.30, f32[]{:T(128)S(6)} %sub.293, f32[]{:T(128)} %bitcast.29, f32[]{:T(128)S(6)} %sub.290, f32[]{:T(128)} %bitcast.28, f32[]{:T(128)} %bitcast.27, f32[]{:T(128)S(6)} %sub.286, f32[]{:T(128)} %bitcast.26, f32[]{:T(128)} %bitcast.25, ...), kind=kLoop, calls=%fused_computation.54 | loop fusion | flops 133152768 | bytes 8454332 | tf_op jit(solution)/shard_map/reduce_sum | solution.py:90
  122.9 2.5 fusion.21
  126.1 7.3 %all-gather = f32[64,1024]{1,0:T(8,128)S(1)} all-gather(f32[16,1024]{1,0:T(8,128)S(1)} %get-tuple-element.110), channel_id=2, replica_groups=mesh['depth'=4,'tile'=8] {'depth'}, dimensions={0}, use_global_device_ids=true | all-gather | bytes 327680 | tf_op jit(solution)/shard_map/all_gather | solution.py:22
  133.7 50.7 %multiply_reduce_fusion.2 = (f32[16,1024]{1,0:T(8,128)S(1)}, f32[64,16,1024]{2,1,0:T(8,128)S(1)}) fusion(f32[64,16,1024]{2,1,0:T(8,128)} %fusion.21, f32[64,16,1024]{2,1,0:T(8,128)} %copy-done.1, f32[]{:T(128)} %bitcast.47, f32[]{:T(128)} %bitcast.46, f32[]{:T(128)} %bitcast.45, f32[]{:T(128)} %bitcast.44, f32[]{:T(128)} %bitcast.43, f32[]{:T(128)} %bitcast.42, ...), kind=kLoop, calls=%fused_computation.18 | loop fusion | flops 159367168 | bytes 42000572 | tf_op jit(solution)/shard_map/reduce_sum | solution.py:89
  184.4 39.8 %multiply_reduce_fusion = f32[16,1024]{1,0:T(8,128)S(1)} fusion(f32[64,16,1024]{2,1,0:T(8,128)S(1)} %copy-done.3, f32[64,16,1024]{2,1,0:T(8,128)S(1)} %copy-done.2, f32[64,16,1024]{2,1,0:T(8,128)S(1)} %get-tuple-element.109, f32[]{:T(128)} %bitcast.81, f32[]{:T(128)} %bitcast.80, f32[]{:T(128)} %bitcast.79, f32[]{:T(128)} %bitcast.78, f32[]{:T(128)} %bitcast.77, ...), kind=kLoop, calls=%fused_computation.16 | loop fusion | flops 140492800 | bytes 16842940 | tf_op jit(solution)/shard_map/reduce_sum | solution.py:89
  224.2 39.8 %multiply_reduce_fusion.1 = f32[16,1024]{1,0:T(8,128)S(1)} fusion(f32[64,16,1024]{2,1,0:T(8,128)S(1)} %copy-done.3, f32[64,16,1024]{2,1,0:T(8,128)S(1)} %copy-done.2, f32[64,16,1024]{2,1,0:T(8,128)S(1)} %get-tuple-element.109, f32[]{:T(128)} %bitcast.64, f32[]{:T(128)} %bitcast.63, f32[]{:T(128)} %bitcast.62, f32[]{:T(128)} %bitcast.61, f32[]{:T(128)} %bitcast.60, ...), kind=kLoop, calls=%fused_computation.17 | loop fusion | flops 140492800 | bytes 16842940 | tf_op jit(solution)/shard_map/reduce_sum | solution.py:89
  264.8 19.7 %reduce-scatter.2.cloned.1.call-done = f32[4,16,256]{2,1,0:T(8,128)} async-done(((f32[4,16,1024]{2,1,0:T(8,128)}), f32[4,16,256]{2,1,0:T(8,128)}) %reduce-scatter.2.cloned.1.call-update) | async-done | bytes 65552 | tf_op jit(solution)/shard_map/reduce_scatter | solution.py:109
  285.2 0.8 slice.514
  (46 shorter events, 10.1 us)
Async XLA Ops:
  6.5 17.1 %copy-start.4 = (s32[16]{0:T(128)S(1)}, s32[16]{0:T(128)}, u32[]{:S(2)}) copy-start(s32[16]{0:T(128)} %param.6) | copy-start | bytes 196
  6.5 277.9 %reduce-scatter.2.cloned.1.call-start = ((), (), s32[]{:S(2)}) async-start(), calls=%async_computation.1 | async-start | bytes 327680 | tf_op jit(solution)/shard_map/reduce_scatter | solution.py:109
  7.3 6.3 %collective-permute-start = (bf16[1,16,1024]{2,1,0:T(8,128)(2,1)S(1)}, bf16[1,16,1024]{2,1,0:T(8,128)(2,1)S(1)}, u32[]{:S(2)}, u32[]{:S(2)}) collective-permute-start(bf16[1,16,1024]{2,1,0:T(8,128)(2,1)S(1)} %get-tuple-element.123), channel_id=1, source_target_pairs={{0,8},{8,16},{16,24},{1,9},{9,17},{17,25},{2,10},{10,18},{18,26},{... | collective-permute-start | bytes 98312 | tf_op jit(solution)/shard_map/ppermute | solution.py:12
  11.0 5.2 %collective-permute-start.1 = (bf16[1,16,1024]{2,1,0:T(8,128)(2,1)S(1)}, bf16[1,16,1024]{2,1,0:T(8,128)(2,1)S(1)}, u32[]{:S(2)}, u32[]{:S(2)}) collective-permute-start(bf16[1,16,1024]{2,1,0:T(8,128)(2,1)S(1)} %get-tuple-element.122), channel_id=1, source_target_pairs={{8,0},{16,8},{24,16},{9,1},{17,9},{25,17},{10,2},{18,10},{26,18},{... | collective-permute-start | bytes 98312 | tf_op jit(solution)/shard_map/ppermute | solution.py:15
  16.7 12.6 %collective-permute-start.3 = (bf16[66,1,1024]{2,1,0:T(2,128)(2,1)S(1)}, bf16[66,1,1024]{2,1,0:T(2,128)(2,1)S(1)}, u32[]{:S(2)}, u32[]{:S(2)}) collective-permute-start(bf16[66,1,1024]{2,1,0:T(2,128)(2,1)S(1)} %get-tuple-element.119), channel_id=1, source_target_pairs={{1,0},{2,1},{3,2},{4,3},{5,4},{6,5},{7,6},{9,8},{10,9},{11,10},{12... | collective-permute-start | bytes 405512 | tf_op jit(solution)/shard_map/ppermute | solution.py:15
  18.9 13.2 %collective-permute-start.2 = (bf16[66,1,1024]{2,1,0:T(2,128)(2,1)S(1)}, bf16[66,1,1024]{2,1,0:T(2,128)(2,1)S(1)}, u32[]{:S(2)}, u32[]{:S(2)}) collective-permute-start(bf16[66,1,1024]{2,1,0:T(2,128)(2,1)S(1)} %get-tuple-element.118), channel_id=1, source_target_pairs={{0,1},{1,2},{2,3},{3,4},{4,5},{5,6},{6,7},{8,9},{9,10},{10,11},{11... | collective-permute-start | bytes 405512 | tf_op jit(solution)/shard_map/ppermute | solution.py:12
  44.0 6.3 %collective-permute-start.5 = (bf16[1,16,1024]{2,1,0:T(8,128)(2,1)S(1)}, bf16[1,16,1024]{2,1,0:T(8,128)(2,1)S(1)}, u32[]{:S(2)}, u32[]{:S(2)}) collective-permute-start(bf16[1,16,1024]{2,1,0:T(8,128)(2,1)S(1)} %get-tuple-element.121), channel_id=1, source_target_pairs={{8,0},{16,8},{24,16},{9,1},{17,9},{25,17},{10,2},{18,10},{26,18},{... | collective-permute-start | bytes 98312 | tf_op jit(solution)/shard_map/ppermute | solution.py:15
  46.3 4.3 %collective-permute-start.4 = (bf16[1,16,1024]{2,1,0:T(8,128)(2,1)S(1)}, bf16[1,16,1024]{2,1,0:T(8,128)(2,1)S(1)}, u32[]{:S(2)}, u32[]{:S(2)}) collective-permute-start(bf16[1,16,1024]{2,1,0:T(8,128)(2,1)S(1)} %get-tuple-element.120), channel_id=1, source_target_pairs={{0,8},{8,16},{16,24},{1,9},{9,17},{17,25},{2,10},{10,18},{18,26},{... | collective-permute-start | bytes 98312 | tf_op jit(solution)/shard_map/ppermute | solution.py:12
  51.0 26.7 %collective-permute-start.7 = (bf16[66,1,1024]{2,1,0:T(2,128)(2,1)S(1)}, bf16[66,1,1024]{2,1,0:T(2,128)(2,1)S(1)}, u32[]{:S(2)}, u32[]{:S(2)}) collective-permute-start(bf16[66,1,1024]{2,1,0:T(2,128)(2,1)S(1)} %get-tuple-element.117), channel_id=1, source_target_pairs={{1,0},{2,1},{3,2},{4,3},{5,4},{6,5},{7,6},{9,8},{10,9},{11,10},{12... | collective-permute-start | bytes 405512 | tf_op jit(solution)/shard_map/ppermute | solution.py:15
  53.0 24.8 %collective-permute-start.6 = (bf16[66,1,1024]{2,1,0:T(2,128)(2,1)S(1)}, bf16[66,1,1024]{2,1,0:T(2,128)(2,1)S(1)}, u32[]{:S(2)}, u32[]{:S(2)}) collective-permute-start(bf16[66,1,1024]{2,1,0:T(2,128)(2,1)S(1)} %get-tuple-element.116), channel_id=1, source_target_pairs={{0,1},{1,2},{2,3},{3,4},{4,5},{5,6},{6,7},{8,9},{9,10},{10,11},{11... | collective-permute-start | bytes 405512 | tf_op jit(solution)/shard_map/ppermute | solution.py:12
  79.6 5.4 %copy-start = (f32[66,18,1024]{2,1,0:T(8,128)}, f32[66,18,1024]{2,1,0:T(8,128)S(1)}, u32[]{:S(2)}) copy-start(f32[66,18,1024]{2,1,0:T(8,128)S(1)} %maximum_convert_fusion.1) | copy-start | bytes 14598148
  122.9 3.2 %copy-start.1 = (f32[64,16,1024]{2,1,0:T(8,128)}, f32[64,16,1024]{2,1,0:T(8,128)S(1)}, u32[]{:S(2)}) copy-start(f32[64,16,1024]{2,1,0:T(8,128)S(1)} %get-tuple-element.111) | copy-start | bytes 12582916
  133.5 50.8 %slice-start = ((s8[6488064]{0:T(1024)(128)(4,1)}), s8[2293760]{0:T(1024)(128)(4,1)S(1)}, s32[]{:S(2)}) async-start(s8[6488064]{0:T(1024)(128)(4,1)} %bitcast.90), calls=%async_computation.2 | async-start | bytes 4587520
  133.6 50.7 %slice-start.1 = ((s8[6488064]{0:T(1024)(128)(4,1)}), s8[4194304]{0:T(1024)(128)(4,1)S(1)}, s32[]{:S(2)}) async-start(s8[6488064]{0:T(1024)(128)(4,1)} %bitcast.90), calls=%async_computation.3 | async-start | bytes 8388608
  133.6 50.7 %copy-start.2 = (f32[64,16,1024]{2,1,0:T(8,128)S(1)}, f32[64,16,1024]{2,1,0:T(8,128)}, u32[]{:S(2)}) copy-start(f32[64,16,1024]{2,1,0:T(8,128)} %copy-done.1) | copy-start | bytes 12582916
  133.6 50.7 %copy-start.3 = (f32[64,16,1024]{2,1,0:T(8,128)S(1)}, f32[64,16,1024]{2,1,0:T(8,128)}, u32[]{:S(2)}) copy-start(f32[64,16,1024]{2,1,0:T(8,128)} %fusion.21) | copy-start | bytes 12582916
Sparse Core Ops, SparseCore 0:
  264.9 19.5 reduce-scatter.1
where the time goes:
time: 297 us; the launch traced here: 293 us
  other arithmetic  183 us (62%)
  between operations  32.6 us (11%)
  waiting for transfers between devices  28.4 us (10%)
  starting transfers between devices  23.7 us (8%)
  local copies, waits for them, and re-layouts  18 us (6%)
  blocking collectives  7.35 us (2%)
    reduce_sum x3, other arithmetic, composite(): jnp.sum(weight * colors[c], axis=0)  130 us
    reduce_sum x1, other arithmetic, composite(): return (brick_color, jnp.sum(extinction, axis=0))  37.9 us
    reduce_scatter x1, waiting for transfers between devices, body(): lax.psum_scatter(weighted, 'depth', scatter_dimension=2, tiled=True)  19.7 us
    ppermute x4, starting transfers between devices, padded(): lax.ppermute(lax.slice_in_dim(block, block.shape[dim] - width, None, axis...  15.4 us
    slice x2, local copies, waits for them, and re-layouts, next_along(): return jnp.pad(center[:, :, 1:], ((0, 0), (0, 0), (0, 1)))  9.69 us
    ppermute x4, starting transfers between devices, padded(): lax.ppermute(lax.slice_in_dim(block, 0, width, axis=dim), axis, backward)  8.28 us
    all_gather x1, blocking collectives, carried_in(): pieces = lax.all_gather(value, axis)  7.35 us
    convert_element_type x1, other arithmetic, body(): smoothed = smooth_block(extended).astype(jnp.bfloat16)  5.96 us
  transfers between devices with their start and end apart: 9, of which 5 were waited for; matrix products, arithmetic and copies ran while one was open for 2% of the time, Pallas kernels for 0%

commit v1 on v0

v1 whole, which is shorter than its diff:
```python
import functools
import math

import jax
import jax.numpy as jnp
import numpy as np
from jax import lax
from jax.experimental import pallas as pl
from jax.experimental.pallas import tpu as pltpu
from jax.sharding import PartitionSpec as P

ZB = 16
CB = 256


def windows(width):
    last = width - 2 * CB
    return [min(max(j * CB - CB // 2, 0), last) for j in range(width // CB)]


def along_y(width, before, after):
    mats, index = [], []
    for j, start in enumerate(windows(width)):
        offset = j * CB - start
        if offset not in index:
            index.append(offset)
            k = np.arange(2 * CB)[:, None] - offset
            n = np.arange(CB)[None, :]
            mats.append(before * (k == n - 1) + after * (k == n + 1))
    return np.stack(mats).astype(jnp.bfloat16)


def window_kind(width):
    kinds = []
    out = []
    for j, start in enumerate(windows(width)):
        offset = j * CB - start
        if offset not in kinds:
            kinds.append(offset)
        out.append(kinds.index(offset))
    return out


def constants(planes, rows, width):
    m = ZB * rows
    a = np.zeros((m, m + 2 * rows + 2 * ZB), np.float32)
    dx = np.zeros((m, m + 2 * ZB), np.float32)
    for z in range(ZB):
        for x in range(rows):
            o = z * rows + x
            c = o + rows
            a[o, c] += 4
            a[o, c - rows] += 1
            a[o, c + rows] += 1
            a[o, c - 1 if x else m + 2 * rows + z] += 1
            a[o, c + 1 if x < rows - 1 else m + 2 * rows + ZB + z] += 1
            dx[o, o - 1 if x else m + z] -= 1
            dx[o, o + 1 if x < rows - 1 else m + ZB + z] += 1
    ae = np.zeros((2 * rows, 6 * rows + 4 * ZB), np.float32)
    low_corner = [ZB - 1, 2 * ZB]
    high_corner = [2 * ZB - 1, 3 * ZB]
    for e in range(2):
        for x in range(rows):
            o = e * rows + x
            c = 3 * rows * e + rows + x
            ae[o, c] += 4
            ae[o, c - rows] += 1
            ae[o, c + rows] += 1
            ae[o, c - 1 if x else 6 * rows + low_corner[e]] += 1
            ae[o, c + 1 if x < rows - 1 else 6 * rows + high_corner[e]] += 1
    be = np.zeros((2, planes, 3 * planes + 4 * ZB), np.float32)
    for s, corner in enumerate((low_corner, high_corner)):
        for z in range(planes):
            be[s, z, z] += 4
            be[s, z, z - 1 if z else planes + corner[0]] += 1
            be[s, z, z + 1 if z < planes - 1 else planes + corner[1]] += 1
            be[s, z, planes + 4 * ZB + z] += 1
            be[s, z, 2 * planes + 4 * ZB + z] += 1
    bf = lambda t: t.astype(jnp.bfloat16)
    return [bf(a), bf(dx), bf(ae), bf(be), along_y(width, 1, 1), along_y(width, -1, 1)]


def dot(a, b):
    return jnp.dot(a, b, preferred_element_type=jnp.float32)


def compute(
    table, mask, vol, zlo, zhi, hlo, hhi, inner, corners, a_m, dx_m, ae_m, be_m, sy_m, dy_m,
    out, field, sm, slo, shi, sf, gx, gy,
):
    planes, rows, width = vol.shape
    kind, starts = window_kind(width), windows(width)
    blocks = len(starts)
    m = ZB * rows
    count = table.shape[1]

    field[0 : 2 * rows] = zlo[...].reshape(2 * rows, width)
    field[2 * rows : (planes + 2) * rows] = vol[...].reshape(planes * rows, width)
    field[(planes + 2) * rows :] = zhi[...].reshape(2 * rows, width)

    def cols(j):
        return slice(j * CB, (j + 1) * CB)

    def win(j):
        return slice(starts[j], starts[j] + 2 * CB)

    for j in range(blocks):
        edge_in = jnp.concatenate(
            [field[0 : 3 * rows, cols(j)], field[(planes + 1) * rows :, cols(j)], corners[:, cols(j)]],
            axis=0,
        )
        edge_own = jnp.concatenate(
            [field[rows : 2 * rows, win(j)], field[(planes + 2) * rows : (planes + 3) * rows, win(j)]],
            axis=0,
        )
        edge = 0.1 * (dot(ae_m[...], edge_in) + dot(edge_own, sy_m[kind[j]]))
        low = (edge[:rows] * mask[0]).astype(jnp.bfloat16)
        high = (edge[rows:] * mask[1]).astype(jnp.bfloat16)
        sm[0:rows, cols(j)] = low
        sm[(planes + 1) * rows :, cols(j)] = high
        sf[0:rows, cols(j)] = low.astype(jnp.float32)
        sf[(planes + 1) * rows :, cols(j)] = high.astype(jnp.float32)
        for s, (near, far, dst) in enumerate(
            ((hlo[1], hlo[0], slo), (hhi[0], hhi[1], shi))
        ):
            side_in = jnp.concatenate(
                [near[:, cols(j)], corners[:, cols(j)], far[:, cols(j)], inner[s, :, cols(j)]], axis=0
            )
            side = 0.1 * (dot(be_m[s], side_in) + dot(near[:, win(j)], sy_m[kind[j]]))
            dst[:, cols(j)] = (side * mask[2 + s]).astype(jnp.bfloat16)

    def smooth(zb, carry):
        first = pl.multiple_of((zb * ZB + 1) * rows, rows)
        own = pl.multiple_of((zb * ZB + 2) * rows, rows)
        put = pl.multiple_of((zb * ZB + 1) * rows, rows)
        zs = pl.ds(pl.multiple_of(zb * ZB, ZB), ZB)
        for j in range(blocks):
            near = jnp.concatenate(
                [field[pl.ds(first, m + 2 * rows), cols(j)], hlo[1, zs, cols(j)], hhi[0, zs, cols(j)]],
                axis=0,
            )
            value = dot(a_m[...], near) + dot(field[pl.ds(own, m), win(j)], sy_m[kind[j]])
            rounded = (0.1 * value).astype(jnp.bfloat16)
            sm[pl.ds(put, m), cols(j)] = rounded
            sf[pl.ds(put, m), cols(j)] = rounded.astype(jnp.float32)
        return carry

    lax.fori_loop(0, planes // ZB, smooth, 0)

    def slopes(zb, carry):
        own = pl.multiple_of((zb * ZB + 1) * rows, rows)
        put = pl.multiple_of(zb * ZB * rows, rows)
        zs = pl.ds(pl.multiple_of(zb * ZB, ZB), ZB)
        for j in range(blocks):
            near = jnp.concatenate(
                [sm[pl.ds(own, m), cols(j)], slo[zs, cols(j)], shi[zs, cols(j)]], axis=0
            )
            gx[pl.ds(put, m), cols(j)] = dot(dx_m[...], near)
            gy[pl.ds(put, m), cols(j)] = dot(sm[pl.ds(own, m), win(j)], dy_m[kind[j]])
        return carry

    lax.fori_loop(0, planes // ZB, slopes, 0)

    halves = rows // 8
    step = 4
    knots = [table[0, k] for k in range(count)]
    drops = [table[4, k] for k in range(count)]
    base = table[5, 3]

    def piece(p, carry):
        row = (p % halves) * 8
        col = pl.ds(pl.multiple_of((p // halves) * 128, 128), 128)

        def at(z):
            return pl.ds(pl.multiple_of(z * rows + row, 8), 8)

        def march(i, state):
            prev, here, tau, through, total, line, *bends = state
            for u in range(step):
                z = i * step + u
                after = sf[at(z + 2), col]
                sx, sy = gx[at(z), col], gy[at(z), col]
                sz = after - prev
                facing = jnp.abs(0.42 * sz + 0.56 * sx)
                shading = 0.3 + facing * lax.rsqrt(sz * sz + sx * sx + (sy * sy + 0.4))
                x = jnp.minimum(jnp.maximum(here, knots[0]), knots[count - 1])
                tops = [jnp.maximum(x, knots[k]) for k in range(1, count - 1)]
                terms = [base + drops[0] * x] + [drops[k] * tops[k - 1] for k in range(1, count - 1)]
                while len(terms) > 1:
                    terms = [
                        terms[t] + terms[t + 1] if t + 1 < len(terms) else terms[t]
                        for t in range(0, len(terms), 2)
                    ]
                tau = tau + terms[0]
                left = jnp.exp2(tau)
                weight = shading * (through - left)
                through = left
                total = total + weight
                line = line + weight * x
                bends = [bends[k] + weight * tops[k] for k in range(count - 2)]
                prev, here = here, after
            return (prev, here, tau, through, total, line, *bends)

        zero = jnp.zeros((8, 128), jnp.float32)
        state = (sf[at(0), col], sf[at(1), col], zero, zero + 1.0) + (zero,) * count
        _, _, tau, _, total, line, *bends = lax.fori_loop(0, planes // step, march, state)
        for c in range(3):
            value = table[5, c] * total + table[1 + c, 0] * line
            for k in range(1, count - 1):
                value = value + table[1 + c, k] * bends[k - 1]
            out[c, pl.ds(row, 8), col] = value
        out[3, pl.ds(row, 8), col] = tau
        return carry

    lax.fori_loop(0, halves * (width // 128), piece, 0)


def transfer_table(knot_pos, knot_color, depth_cells):
    at = (knot_pos.astype(jnp.float32) - 127.5) / 70.0
    scale = jnp.array([1 / 255.0] * 3 + [-4.0 * math.log2(math.e) / depth_cells / 255.0], jnp.float32)
    value = knot_color.astype(jnp.float32) * scale[:, None]
    slope = (value[:, 1:] - value[:, :-1]) / (at[1:] - at[:-1])
    bend = jnp.concatenate([slope[:, :1], slope[:, 1:] - slope[:, :-1]], axis=1)
    bend = jnp.pad(bend, ((0, 0), (0, 1)))
    const = value[:, 0] - jnp.sum(bend * at[None], axis=1)
    const = jnp.pad(const, (0, at.shape[0] - 4))
    return jnp.concatenate([at[None], bend, const[None]], axis=0)


def shift(value, axes, sizes, steps):
    pairs = []
    for i in range(sizes[0]):
        for j in range(sizes[1]):
            k, l = i + steps[0], j + steps[1]
            if 0 <= k < sizes[0] and 0 <= l < sizes[1]:
                pairs.append((i * sizes[1] + j, k * sizes[1] + l))
    return lax.ppermute(value, axes, pairs)


def solution(mesh):
    axes = ("depth", "tile")
    sizes = tuple(mesh.shape[a] for a in axes)

    def body(volume, knot_pos, knot_color):
        planes, rows, width = volume.shape
        go = functools.partial(shift, axes=axes, sizes=sizes)
        zlo = go(volume[planes - 2 :], steps=(1, 0))
        zhi = go(volume[:2], steps=(-1, 0))
        first = jnp.transpose(volume[:, :2], (1, 0, 2))
        last = jnp.transpose(volume[:, rows - 2 :], (1, 0, 2))
        hlo = go(last, steps=(0, 1))
        hhi = go(first, steps=(0, -1))
        inner = jnp.stack([first[0], last[1]])
        corners = jnp.concatenate(
            [
                go(last[1, planes - ZB :], steps=(1, 1)),
                go(first[0, planes - ZB :], steps=(1, -1)),
                go(last[1, :ZB], steps=(-1, 1)),
                go(first[0, :ZB], steps=(-1, -1)),
            ],
            axis=0,
        )
        d, t = lax.axis_index("depth"), lax.axis_index("tile")
        mask = jnp.stack([d > 0, d < sizes[0] - 1, t > 0, t < sizes[1] - 1]).astype(jnp.float32)
        table = transfer_table(knot_pos, knot_color, planes * sizes[0])
        consts = [jnp.asarray(c) for c in constants(planes, rows, width)]
        smem = pl.BlockSpec(memory_space=pltpu.SMEM)
        vmem = pl.BlockSpec(memory_space=pltpu.VMEM)
        brick = pl.pallas_call(
            compute,
            out_shape=jax.ShapeDtypeStruct((4, rows, width), jnp.float32),
            in_specs=[smem, smem] + [vmem] * (7 + len(consts)),
            out_specs=vmem,
            scratch_shapes=[
                pltpu.VMEM(((planes + 4) * rows, width), jnp.bfloat16),
                pltpu.VMEM(((planes + 2) * rows, width), jnp.bfloat16),
                pltpu.VMEM((planes, width), jnp.bfloat16),
                pltpu.VMEM((planes, width), jnp.bfloat16),
                pltpu.VMEM(((planes + 2) * rows, width), jnp.float32),
                pltpu.VMEM((planes * rows, width), jnp.float32),
                pltpu.VMEM((planes * rows, width), jnp.float32),
            ],
            compiler_params=pltpu.CompilerParams(vmem_limit_bytes=48 << 20),
        )(table, mask, volume, zlo, zhi, hlo, hhi, inner, corners, *consts)
        part = width // sizes[0]
        split = brick.reshape(4, rows, sizes[0], part)
        parts = lax.all_to_all(split, "depth", split_axis=2, concat_axis=0, tiled=False)
        colors = jnp.zeros((3, rows, part), jnp.float32)
        ahead = jnp.zeros((rows, part), jnp.float32)
        for i in range(sizes[0]):
            colors = colors + parts[i, :3] * jnp.exp2(ahead)[None]
            ahead = ahead + parts[i, 3]
        return jnp.concatenate([colors, (1.0 - jnp.exp2(ahead))[None]], axis=0)

    in_specs = (P("depth", "tile", None), P(), P())
    return jax.shard_map(
        body, mesh=mesh, in_specs=in_specs, out_specs=P(None, "tile", "depth"), check_vma=False
    )
```

time: 297 us -> 78.5 us (0.26)
  the two profiles are of different devices: /device:TPU:21 before, /device:TPU:8 now
where the time goes in v1:
time: 78.5 us; the launch traced here: 77.7 us
  Pallas kernels  25.3 us (32%)
  starting transfers between devices  22.2 us (28%)
  local copies, waits for them, and re-layouts  13.9 us (18%)
  blocking collectives  10 us (13%)
  waiting for transfers between devices  3.93 us (5%)
  other arithmetic  2.09 us (3%)
    pallas_call x1, Pallas kernels, body(): pl.pallas_call(compute, out_shape=jax.ShapeDtypeStruct((4, rows, width),...  25.3 us
    ppermute x8, starting transfers between devices, shift(): return lax.ppermute(value, axes, pairs)  22.2 us
    all_to_all x1, blocking collectives, body(): lax.all_to_all(split, 'depth', split_axis=2, concat_axis=0, tiled=False)  10 us
    unnamed x26, local copies, waits for them, and re-layouts  6.16 us
    ppermute x8, waiting for transfers between devices, shift(): return lax.ppermute(value, axes, pairs)  3.93 us
    slice x1, local copies, waits for them, and re-layouts, body(): first = jnp.transpose(volume[:, :2], (1, 0, 2))  2.15 us
    slice x2, local copies, waits for them, and re-layouts, body(): inner = jnp.stack([first[0], last[1]])  1.83 us
  transfers between devices with their start and end apart: 8, of which 1 were waited for; matrix products, arithmetic and copies ran while one was open for 10% of the time, Pallas kernels for 0%

profile of v1, /device:TPU:8, one launch (start us, length us, event | category | flops | bytes accessed | tf_op | source)
XLA Modules:
  0.0 77.7 jit_solution(3203112193833741399)
XLA Ops:
  0.1 2.1 %fusion.11 = (bf16[64,2,1024]{2,1,0:T(2,128)(2,1)S(1)}, bf16[64,2,1024]{2,1,0:T(2,128)(2,1)S(1)}) fusion(bf16[64,16,1024]{2,1,0:T(8,128)(2,1)} %vol.1), kind=kLoop, calls=%fused_computation.42 | loop fusion | bytes 1048576 | tf_op jit(solution)/shard_map/slice | solution.py:249
  2.2 0.7 copy.25
  3.0 3.4 %collective-permute-start.2 = (bf16[2,64,1024]{2,1,0:T(8,128)(2,1)}, bf16[2,64,1024]{2,1,0:T(8,128)(2,1)S(1)}, u32[]{:S(2)}, u32[]{:S(2)}) collective-permute-start(bf16[2,64,1024]{2,1,0:T(8,128)(2,1)} %bitcast.60), channel_id=1, source_target_pairs={{0,1},{1,2},{2,3},{3,4},{4,5},{5,6},{6,7},{8,9},{9,10},{10,11},{11... | collective-permute-start | bytes 786440 | tf_op jit(solution)/shard_map/ppermute | solution.py:237
  6.4 1.4 %slice_bitcast_fusion.7 = (bf16[16,1024]{1,0:T(8,128)(2,1)}, bf16[16,1024]{1,0:T(8,128)(2,1)S(1)}) fusion(bf16[2,64,1024]{2,1,0:T(8,128)(2,1)} %bitcast.60), kind=kLoop, calls=%fused_computation.18 | loop fusion | bytes 131072 | tf_op jit(solution)/shard_map/squeeze | solution.py:256
  7.8 3.2 %collective-permute-start.4 = (bf16[16,1024]{1,0:T(8,128)(2,1)}, bf16[16,1024]{1,0:T(8,128)(2,1)}, u32[]{:S(2)}, u32[]{:S(2)}) collective-permute-start(bf16[16,1024]{1,0:T(8,128)(2,1)} %get-tuple-element.15), channel_id=1, source_target_pairs={{0,9},{1,10},{2,11},{3,12},{4,13},{5,14},{6,15},{8,17},{9,18},{10,... | collective-permute-start | bytes 98312 | tf_op jit(solution)/shard_map/ppermute | solution.py:237
  11.0 0.8 copy.24
  11.7 3.3 %collective-permute-start.3 = (bf16[2,64,1024]{2,1,0:T(8,128)(2,1)}, bf16[2,64,1024]{2,1,0:T(8,128)(2,1)}, u32[]{:S(2)}, u32[]{:S(2)}) collective-permute-start(bf16[2,64,1024]{2,1,0:T(8,128)(2,1)} %bitcast.59), channel_id=1, source_target_pairs={{1,0},{2,1},{3,2},{4,3},{5,4},{6,5},{7,6},{9,8},{10,9},{11,10},{12... | collective-permute-start | bytes 786440 | tf_op jit(solution)/shard_map/ppermute | solution.py:237
  15.0 1.4 %slice_bitcast_fusion.6 = (bf16[16,1024]{1,0:T(8,128)(2,1)}, bf16[16,1024]{1,0:T(8,128)(2,1)}) fusion(bf16[2,64,1024]{2,1,0:T(8,128)(2,1)} %bitcast.59), kind=kLoop, calls=%fused_computation.17 | loop fusion | bytes 131072 | tf_op jit(solution)/shard_map/squeeze | solution.py:257
  16.5 4.2 %collective-permute-start.5 = (bf16[16,1024]{1,0:T(8,128)(2,1)}, bf16[16,1024]{1,0:T(8,128)(2,1)}, u32[]{:S(2)}, u32[]{:S(2)}) collective-permute-start(bf16[16,1024]{1,0:T(8,128)(2,1)} %get-tuple-element.17), channel_id=1, source_target_pairs={{1,8},{2,9},{3,10},{4,11},{5,12},{6,13},{7,14},{9,16},{10,17},{11,... | collective-permute-start | bytes 98312 | tf_op jit(solution)/shard_map/ppermute | solution.py:237
  20.7 1.3 %collective-permute-start.6 = (bf16[16,1024]{1,0:T(8,128)(2,1)S(1)}, bf16[16,1024]{1,0:T(8,128)(2,1)}, u32[]{:S(2)}, u32[]{:S(2)}) collective-permute-start(bf16[16,1024]{1,0:T(8,128)(2,1)S(1)} %get-tuple-element.16), channel_id=1, source_target_pairs={{8,1},{9,2},{10,3},{11,4},{12,5},{13,6},{14,7},{16,9},{17,10},{18,... | collective-permute-start | bytes 98312 | tf_op jit(solution)/shard_map/ppermute | solution.py:237
  22.0 0.9 %slice.104 = bf16[1,64,1024]{2,1,0:T(8,128)(2,1)S(1)} slice(bf16[2,64,1024]{2,1,0:T(8,128)(2,1)} %bitcast.59), slice={[0:1], [0:64], [0:1024]} | slice | bytes 262144 | tf_op jit(solution)/shard_map/slice | solution.py:253
  22.9 0.9 %slice.105 = bf16[1,64,1024]{2,1,0:T(8,128)(2,1)S(1)} slice(bf16[2,64,1024]{2,1,0:T(8,128)(2,1)} %bitcast.60), slice={[1:2], [0:64], [0:1024]} | slice | bytes 262144 | tf_op jit(solution)/shard_map/slice | solution.py:253
  25.2 1.3 %collective-permute-start.7 = (bf16[16,1024]{1,0:T(8,128)(2,1)}, bf16[16,1024]{1,0:T(8,128)(2,1)S(1)}, u32[]{:S(2)}, u32[]{:S(2)}) collective-permute-start(bf16[16,1024]{1,0:T(8,128)(2,1)} %get-tuple-element.18), channel_id=1, source_target_pairs={{9,0},{10,1},{11,2},{12,3},{13,4},{14,5},{15,6},{17,8},{18,9},{19,... | collective-permute-start | bytes 98312 | tf_op jit(solution)/shard_map/ppermute | solution.py:237
  26.6 4.2 %collective-permute-start = (bf16[2,16,1024]{2,1,0:T(8,128)(2,1)}, bf16[2,16,1024]{2,1,0:T(8,128)(2,1)S(1)}, u32[]{:S(2)}, u32[]{:S(2)}) collective-permute-start(bf16[2,16,1024]{2,1,0:T(8,128)(2,1)} %get-tuple-element.10), channel_id=1, source_target_pairs={{0,8},{1,9},{2,10},{3,11},{4,12},{5,13},{6,14},{7,15},{8,16},{9,17... | collective-permute-start | bytes 196616 | tf_op jit(solution)/shard_map/ppermute | solution.py:237
  30.8 1.3 %collective-permute-start.1 = (bf16[2,16,1024]{2,1,0:T(8,128)(2,1)}, bf16[2,16,1024]{2,1,0:T(8,128)(2,1)S(1)}, u32[]{:S(2)}, u32[]{:S(2)}) collective-permute-start(bf16[2,16,1024]{2,1,0:T(8,128)(2,1)} %get-tuple-element.9), channel_id=1, source_target_pairs={{8,0},{9,1},{10,2},{11,3},{12,4},{13,5},{14,6},{15,7},{16,8},{17,9... | collective-permute-start | bytes 196616 | tf_op jit(solution)/shard_map/ppermute | solution.py:237
  32.1 0.8 %pad_maximum_fusion.1.corners = bf16[64,1024]{1,0:T(8,128)(2,1)S(1)} fusion(bf16[16,1024]{1,0:T(8,128)(2,1)S(1)} %collective-permute-done.7, bf16[16,1024]{1,0:T(8,128)(2,1)} %collective-permute-done.6, bf16[16,1024]{1,0:T(8,128)(2,1)} %collective-permute-done.5, bf16[16,1024]{1,0:T(8,128)(2,1)} %collective-permute-done.4), kind=kLoop, calls=%fused_computation.3 | loop fusion | flops 524288 | bytes 262144 | tf_op jit(solution)/shard_map/concatenate | solution.py:254
  32.9 3.9 %collective-permute-done.1.zhi = bf16[2,16,1024]{2,1,0:T(8,128)(2,1)S(1)} collective-permute-done((bf16[2,16,1024]{2,1,0:T(8,128)(2,1)}, bf16[2,16,1024]{2,1,0:T(8,128)(2,1)S(1)}, u32[]{:S(2)}, u32[]{:S(2)}) %collective-permute-start.1) | collective-permute-done | bytes 65568 | tf_op jit(solution)/shard_map/ppermute | solution.py:237
  36.8 0.7 copy-done.3
  37.5 1.1 %copy-done.2 = bf16[3,512,256]{2,1,0:T(8,128)(2,1)S(1)} copy-done((bf16[3,512,256]{2,1,0:T(8,128)(2,1)S(1)}, bf16[3,512,256]{2,1,0:T(8,128)(2,1)}, u32[]{:S(2)}) %copy-start.2) | copy-done | bytes 786456
  38.7 0.9 %copy-done.4 = bf16[2,64,1024]{2,1,0:T(8,128)(2,1)S(1)} copy-done((bf16[2,64,1024]{2,1,0:T(8,128)(2,1)S(1)}, bf16[2,64,1024]{2,1,0:T(8,128)(2,1)}, u32[]{:S(2)}) %copy-start.4) | copy-done | bytes 262168
  39.6 0.9 %copy-done.5 = bf16[256,320]{1,0:T(8,128)(2,1)S(1)} copy-done((bf16[256,320]{1,0:T(8,128)(2,1)S(1)}, bf16[256,320]{1,0:T(8,128)(2,1)}, u32[]{:S(2)}) %copy-start.5) | copy-done | bytes 163864
  40.5 0.9 %copy-done.6 = bf16[256,288]{1,0:T(8,128)(2,1)S(1)} copy-done((bf16[256,288]{1,0:T(8,128)(2,1)S(1)}, bf16[256,288]{1,0:T(8,128)(2,1)}, u32[]{:S(2)}) %copy-start.6) | copy-done | bytes 147480
  41.5 25.3 %shard_map.100 = f32[4,16,1024]{2,1,0:T(8,128)S(1)} custom-call(f32[6,16]{1,0:T(8,128)S(1)} %pad_maximum_fusion.3.table, f32[4]{0:T(128)S(1)} %add_convert_fusion.mask, bf16[64,16,1024]{2,1,0:T(8,128)(2,1)S(1)} %copy-done, bf16[2,16,1024]{2,1,0:T(8,128)(2,1)S(1)} %collective-permute-done.zlo, bf16[2,16,1024]{2,1,0:T(8,128)(2,1)S(1)} %collective-permute-done.1.zhi, ...), custom_call_target="tpu_custom_call" | custom-call | tf_op jit(solution)/shard_map/pallas_call | solution.py:269
  67.0 10.0 %all_to_all.15 = f32[1,4,16,4,256]{4,2,1,0,3:T(8,128)S(1)} all-to-all(f32[1,4,16,4,256]{4,2,1,0,3:T(8,128)S(1)} %copy.19), channel_id=1, replica_groups=mesh['depth'=4,'tile'=8] {'depth'}, dimensions={3} | all-to-all | bytes 524288 | tf_op jit(solution)/shard_map/all_to_all | solution.py:287
  (44 shorter events, 2.3 us)
Async XLA Ops:
  0.0 24.6 %copy-start.10 = (f32[4]{0:T(128)S(1)}, f32[4]{0:T(128)}, u32[]{:S(2)}) copy-start(f32[4]{0:T(128)} %constant.41.clone) | copy-start | bytes 52
  0.0 37.5 %copy-start.8 = (bf16[32,160]{1,0:T(8,128)(2,1)S(1)}, bf16[32,160]{1,0:T(8,128)(2,1)}, u32[]{:S(2)}) copy-start(bf16[32,160]{1,0:T(8,128)(2,1)} %constant.44.clone.ae_m) | copy-start | bytes 30724
  0.0 37.5 %copy-start.1 = (bf16[3,512,256]{2,1,0:T(8,128)(2,1)S(1)}, bf16[3,512,256]{2,1,0:T(8,128)(2,1)}, u32[]{:S(2)}) copy-start(bf16[3,512,256]{2,1,0:T(8,128)(2,1)} %constant.46.clone.sy_m) | copy-start | bytes 2359300
  0.0 23.8 %copy-start = (bf16[64,16,1024]{2,1,0:T(8,128)(2,1)S(1)}, bf16[64,16,1024]{2,1,0:T(8,128)(2,1)}, u32[]{:S(2)}) copy-start(bf16[64,16,1024]{2,1,0:T(8,128)(2,1)} %vol.1) | copy-start | bytes 6291460
  0.0 37.5 %copy-start.7 = (bf16[2,64,256]{2,1,0:T(8,128)(2,1)S(1)}, bf16[2,64,256]{2,1,0:T(8,128)(2,1)}, u32[]{:S(2)}) copy-start(bf16[2,64,256]{2,1,0:T(8,128)(2,1)} %constant.45.clone.be_m) | copy-start | bytes 196612
  0.0 24.4 %copy-start.11 = (s32[16]{0:T(128)S(1)}, s32[16]{0:T(128)}, u32[]{:S(2)}) copy-start(s32[16]{0:T(128)} %param.11) | copy-start | bytes 196
  0.0 24.5 %copy-start.9 = (s32[4,16]{1,0:T(4,128)S(1)}, s32[4,16]{1,0:T(4,128)}, u32[]{:S(2)}) copy-start(s32[4,16]{1,0:T(4,128)} %param.12) | copy-start | bytes 772
  3.0 33.8 %collective-permute-start.2 = (bf16[2,64,1024]{2,1,0:T(8,128)(2,1)}, bf16[2,64,1024]{2,1,0:T(8,128)(2,1)S(1)}, u32[]{:S(2)}, u32[]{:S(2)}) collective-permute-start(bf16[2,64,1024]{2,1,0:T(8,128)(2,1)} %bitcast.60), channel_id=1, source_target_pairs={{0,1},{1,2},{2,3},{3,4},{4,5},{5,6},{6,7},{8,9},{9,10},{10,11},{11... | collective-permute-start | bytes 786440 | tf_op jit(solution)/shard_map/ppermute | solution.py:237
  7.8 17.4 %collective-permute-start.4 = (bf16[16,1024]{1,0:T(8,128)(2,1)}, bf16[16,1024]{1,0:T(8,128)(2,1)}, u32[]{:S(2)}, u32[]{:S(2)}) collective-permute-start(bf16[16,1024]{1,0:T(8,128)(2,1)} %get-tuple-element.15), channel_id=1, source_target_pairs={{0,9},{1,10},{2,11},{3,12},{4,13},{5,14},{6,15},{8,17},{9,18},{10,... | collective-permute-start | bytes 98312 | tf_op jit(solution)/shard_map/ppermute | solution.py:237
  11.7 25.8 %collective-permute-start.3 = (bf16[2,64,1024]{2,1,0:T(8,128)(2,1)}, bf16[2,64,1024]{2,1,0:T(8,128)(2,1)}, u32[]{:S(2)}, u32[]{:S(2)}) collective-permute-start(bf16[2,64,1024]{2,1,0:T(8,128)(2,1)} %bitcast.59), channel_id=1, source_target_pairs={{1,0},{2,1},{3,2},{4,3},{5,4},{6,5},{7,6},{9,8},{10,9},{11,10},{12... | collective-permute-start | bytes 786440 | tf_op jit(solution)/shard_map/ppermute | solution.py:237
  16.5 10.1 %collective-permute-start.5 = (bf16[16,1024]{1,0:T(8,128)(2,1)}, bf16[16,1024]{1,0:T(8,128)(2,1)}, u32[]{:S(2)}, u32[]{:S(2)}) collective-permute-start(bf16[16,1024]{1,0:T(8,128)(2,1)} %get-tuple-element.17), channel_id=1, source_target_pairs={{1,8},{2,9},{3,10},{4,11},{5,12},{6,13},{7,14},{9,16},{10,17},{11,... | collective-permute-start | bytes 98312 | tf_op jit(solution)/shard_map/ppermute | solution.py:237
  20.7 10.1 %collective-permute-start.6 = (bf16[16,1024]{1,0:T(8,128)(2,1)S(1)}, bf16[16,1024]{1,0:T(8,128)(2,1)}, u32[]{:S(2)}, u32[]{:S(2)}) collective-permute-start(bf16[16,1024]{1,0:T(8,128)(2,1)S(1)} %get-tuple-element.16), channel_id=1, source_target_pairs={{8,1},{9,2},{10,3},{11,4},{12,5},{13,6},{14,7},{16,9},{17,10},{18,... | collective-permute-start | bytes 98312 | tf_op jit(solution)/shard_map/ppermute | solution.py:237
  25.2 6.9 %collective-permute-start.7 = (bf16[16,1024]{1,0:T(8,128)(2,1)}, bf16[16,1024]{1,0:T(8,128)(2,1)S(1)}, u32[]{:S(2)}, u32[]{:S(2)}) collective-permute-start(bf16[16,1024]{1,0:T(8,128)(2,1)} %get-tuple-element.18), channel_id=1, source_target_pairs={{9,0},{10,1},{11,2},{12,3},{13,4},{14,5},{15,6},{17,8},{18,9},{19,... | collective-permute-start | bytes 98312 | tf_op jit(solution)/shard_map/ppermute | solution.py:237
  26.6 6.3 %collective-permute-start = (bf16[2,16,1024]{2,1,0:T(8,128)(2,1)}, bf16[2,16,1024]{2,1,0:T(8,128)(2,1)S(1)}, u32[]{:S(2)}, u32[]{:S(2)}) collective-permute-start(bf16[2,16,1024]{2,1,0:T(8,128)(2,1)} %get-tuple-element.10), channel_id=1, source_target_pairs={{0,8},{1,9},{2,10},{3,11},{4,12},{5,13},{6,14},{7,15},{8,16},{9,17... | collective-permute-start | bytes 196616 | tf_op jit(solution)/shard_map/ppermute | solution.py:237
  30.8 6.0 %collective-permute-start.1 = (bf16[2,16,1024]{2,1,0:T(8,128)(2,1)}, bf16[2,16,1024]{2,1,0:T(8,128)(2,1)S(1)}, u32[]{:S(2)}, u32[]{:S(2)}) collective-permute-start(bf16[2,16,1024]{2,1,0:T(8,128)(2,1)} %get-tuple-element.9), channel_id=1, source_target_pairs={{8,0},{9,1},{10,2},{11,3},{12,4},{13,5},{14,6},{15,7},{16,8},{17,9... | collective-permute-start | bytes 196616 | tf_op jit(solution)/shard_map/ppermute | solution.py:237
  36.8 0.7 copy-start.3
  37.5 1.1 %copy-start.2 = (bf16[3,512,256]{2,1,0:T(8,128)(2,1)S(1)}, bf16[3,512,256]{2,1,0:T(8,128)(2,1)}, u32[]{:S(2)}) copy-start(bf16[3,512,256]{2,1,0:T(8,128)(2,1)} %constant.47.clone.dy_m) | copy-start | bytes 2359300
  38.7 0.9 %copy-start.4 = (bf16[2,64,1024]{2,1,0:T(8,128)(2,1)S(1)}, bf16[2,64,1024]{2,1,0:T(8,128)(2,1)}, u32[]{:S(2)}) copy-start(bf16[2,64,1024]{2,1,0:T(8,128)(2,1)} %copy-done.3) | copy-start | bytes 786436
  39.6 0.9 %copy-start.5 = (bf16[256,320]{1,0:T(8,128)(2,1)S(1)}, bf16[256,320]{1,0:T(8,128)(2,1)}, u32[]{:S(2)}) copy-start(bf16[256,320]{1,0:T(8,128)(2,1)} %constant.42.clone.a_m) | copy-start | bytes 491524
  40.5 0.9 %copy-start.6 = (bf16[256,288]{1,0:T(8,128)(2,1)S(1)}, bf16[256,288]{1,0:T(8,128)(2,1)}, u32[]{:S(2)}) copy-start(bf16[256,288]{1,0:T(8,128)(2,1)} %constant.43.clone.dx_m) | copy-start | bytes 442372

commit v2 on v1

v2 whole, which is shorter than its diff:
```python
import functools
import math

import jax
import jax.numpy as jnp
import numpy as np
from jax import lax
from jax.experimental import pallas as pl
from jax.experimental.pallas import tpu as pltpu
from jax.sharding import PartitionSpec as P

ZB = 16
CB = 256


def windows(width):
    last = width - 2 * CB
    return [min(max(j * CB - CB // 2, 0), last) for j in range(width // CB)]


def along_y(width, before, after):
    mats, index = [], []
    for j, start in enumerate(windows(width)):
        offset = j * CB - start
        if offset not in index:
            index.append(offset)
            k = np.arange(2 * CB)[:, None] - offset
            n = np.arange(CB)[None, :]
            mats.append(before * (k == n - 1) + after * (k == n + 1))
    return np.stack(mats).astype(jnp.bfloat16)


def window_kind(width):
    kinds = []
    out = []
    for j, start in enumerate(windows(width)):
        offset = j * CB - start
        if offset not in kinds:
            kinds.append(offset)
        out.append(kinds.index(offset))
    return out


def constants(planes, rows, width):
    m = ZB * rows
    a = np.zeros((m, m + 2 * rows + 2 * ZB), np.float32)
    dx = np.zeros((m, m + 2 * ZB), np.float32)
    for z in range(ZB):
        for x in range(rows):
            o = z * rows + x
            c = o + rows
            a[o, c] += 4
            a[o, c - rows] += 1
            a[o, c + rows] += 1
            a[o, c - 1 if x else m + 2 * rows + z] += 1
            a[o, c + 1 if x < rows - 1 else m + 2 * rows + ZB + z] += 1
            dx[o, o - 1 if x else m + z] -= 1
            dx[o, o + 1 if x < rows - 1 else m + ZB + z] += 1
    ae = np.zeros((2 * rows, 6 * rows + 4 * ZB), np.float32)
    low_corner = [ZB - 1, 2 * ZB]
    high_corner = [2 * ZB - 1, 3 * ZB]
    for e in range(2):
        for x in range(rows):
            o = e * rows + x
            c = 3 * rows * e + rows + x
            ae[o, c] += 4
            ae[o, c - rows] += 1
            ae[o, c + rows] += 1
            ae[o, c - 1 if x else 6 * rows + low_corner[e]] += 1
            ae[o, c + 1 if x < rows - 1 else 6 * rows + high_corner[e]] += 1
    be = np.zeros((2, planes, 3 * planes + 4 * ZB), np.float32)
    for s, corner in enumerate((low_corner, high_corner)):
        for z in range(planes):
            be[s, z, z] += 4
            be[s, z, z - 1 if z else planes + corner[0]] += 1
            be[s, z, z + 1 if z < planes - 1 else planes + corner[1]] += 1
            be[s, z, planes + 4 * ZB + z] += 1
            be[s, z, 2 * planes + 4 * ZB + z] += 1
    pack = np.zeros((4 * ZB, m), np.float32)
    for r, row in enumerate((0, 1, rows - 2, rows - 1)):
        for z in range(ZB):
            pack[r * ZB + z, z * rows + row] = 1
    bf = lambda t: t.astype(jnp.bfloat16)
    return [bf(pack), along_y(width, 1, 1), bf(a), bf(ae), bf(be), bf(dx), along_y(width, -1, 1)]


def dot(a, b):
    return jnp.dot(a, b, preferred_element_type=jnp.float32)


def compute(
    sizes, knot_pos, knot_color, vol,
    pack_h, sy_h, a_h, ae_h, be_h, dx_h, dy_h,
    out, field, packed, hlo, hhi, corners, sm, slo, shi, sf, gx, gy, tab, stage, parts,
    pack_m, sy_m, a_m, ae_m, be_m, dx_m, dy_m,
    vol_sem, const_sem, z_send, z_recv, x_send, x_recv, c_send, c_recv, f_send, f_recv,
):
    rows, width = out.shape[1], vol.shape[1]
    planes = vol.shape[0] // rows
    depths, tiles = sizes
    d, t = lax.axis_index("depth"), lax.axis_index("tile")
    kind, starts = window_kind(width), windows(width)
    blocks = len(starts)
    groups = planes // ZB
    m = ZB * rows
    count = knot_pos.shape[0]

    loads = []
    for zb in range(groups):
        loads.append(
            pltpu.make_async_copy(
                vol.at[pl.ds(zb * m, m)],
                field.at[pl.ds(2 * rows + zb * m, m)],
                vol_sem.at[zb],
            )
        )
    fetches = [
        pltpu.make_async_copy(src, dst, const_sem.at[i])
        for i, (src, dst) in enumerate(
            (
                (pack_h, pack_m), (sy_h, sy_m), (a_h, a_m), (ae_h, ae_m),
                (be_h, be_m), (dx_h, dx_m), (dy_h, dy_m),
            )
        )
    ]
    fetches[0].start()
    for copy in loads + fetches[1:]:
        copy.start()

    barrier = pltpu.get_barrier_semaphore()

    def hello(depth, tile):
        pl.semaphore_signal(
            barrier, inc=1, device_id=(depth, tile), device_id_type=pl.DeviceIdType.MESH
        )

    lower, upper = t > 0, t < tiles - 1
    nearer, farther = d > 0, d < depths - 1
    near_d, far_d = jnp.maximum(d - 1, 0), jnp.minimum(d + 1, depths - 1)
    low_t, up_t = jnp.maximum(t - 1, 0), jnp.minimum(t + 1, tiles - 1)
    for k in range(1, depths):
        hello(lax.rem(d + k, depths), t)
    for there, tile in ((lower, low_t), (upper, up_t)):
        pl.when(there)(functools.partial(hello, d, tile))
        pl.when(there & nearer)(functools.partial(hello, near_d, tile))
        pl.when(there & farther)(functools.partial(hello, far_d, tile))
    number = lambda flag: jnp.where(flag, 1, 0)
    greeted = (depths - 1) + (number(lower) + number(upper)) * (
        1 + number(nearer) + number(farther)
    )

    def splat(value):
        return jnp.full((8, 128), value, jnp.int32).astype(jnp.float32)

    at = [(splat(knot_pos[k]) - 127.5) * (1.0 / 70.0) for k in range(count)]
    gaps = [1.0 / (at[k + 1] - at[k]) for k in range(count - 1)]
    for k in range(count):
        tab[k] = at[k]
    scales = [1 / 255.0] * 3 + [-4.0 * math.log2(math.e) / (planes * depths) / 255.0]
    for c in range(4):
        value = [splat(knot_color[c, k]) * scales[c] for k in range(count)]
        const, before = value[0], None
        for k in range(count - 1):
            slope = (value[k + 1] - value[k]) * gaps[k]
            bend = slope if k == 0 else slope - before
            before = slope
            const = const - bend * at[k]
            tab[count * (c + 1) + k] = bend
        tab[count * (c + 1) + count - 1] = const

    def cols(j):
        return slice(j * CB, (j + 1) * CB)

    def win(j):
        return slice(starts[j], starts[j] + 2 * CB)

    fetches[0].wait()
    for zb in range(groups):
        loads[zb].wait()
        for j in range(blocks):
            picked = dot(pack_m[...], field[2 * rows + zb * m : 2 * rows + (zb + 1) * m, cols(j)])
            picked = picked.astype(jnp.bfloat16)
            for r in range(4):
                packed[r, zb * ZB : (zb + 1) * ZB, cols(j)] = picked[r * ZB : (r + 1) * ZB]

    pl.semaphore_wait(barrier, greeted)

    def remote(src, dst, send, recv, depth, tile):
        return pltpu.make_async_remote_copy(
            src_ref=src, dst_ref=dst, send_sem=send, recv_sem=recv,
            device_id=(depth, tile), device_id_type=pl.DeviceIdType.MESH,
        )

    inside, end = 2 * rows, (planes + 2) * rows
    z_copies, x_copies, c_copies = [], [], []
    for i, (src, dst, depth, sends, receives) in enumerate(
        (
            (end - 2 * rows, 0, far_d, farther, nearer),
            (inside, end, near_d, nearer, farther),
        )
    ):
        target = field.at[pl.ds(dst, 2 * rows)]
        z_copies.append(
            (
                remote(
                    field.at[pl.ds(src, 2 * rows)], target,
                    z_send.at[i], z_recv.at[i], depth, t,
                ),
                sends, receives, target,
            )
        )
    for zb in range(groups):
        zs = pl.ds(zb * ZB, ZB)
        for i, (src, halo, tile, sends, receives) in enumerate(
            ((2, hlo, up_t, upper, lower), (0, hhi, low_t, lower, upper))
        ):
            target = halo.at[:, zs]
            n = 2 * zb + i
            x_copies.append(
                (
                    remote(
                        packed.at[pl.ds(src, 2), zs], target,
                        x_send.at[n], x_recv.at[n], d, tile,
                    ),
                    sends, receives, target,
                )
            )
    for i, (row, z, depth, tile, sends, receives) in enumerate(
        (
            (3, planes - ZB, far_d, up_t, farther & upper, nearer & lower),
            (0, planes - ZB, far_d, low_t, farther & lower, nearer & upper),
            (3, 0, near_d, up_t, nearer & upper, farther & lower),
            (0, 0, near_d, low_t, nearer & lower, farther & upper),
        )
    ):
        target = corners.at[pl.ds(i * ZB, ZB)]
        c_copies.append(
            (
                remote(
                    packed.at[row, pl.ds(z, ZB)], target,
                    c_send.at[i], c_recv.at[i], depth, tile,
                ),
                sends, receives, target,
            )
        )
    for copy, sends, receives, target in z_copies + x_copies + c_copies:
        pl.when(sends)(copy.start)

    for copy, sends, receives, target in z_copies + x_copies + c_copies:

        @pl.when(jnp.logical_not(receives))
        def _():
            target[...] = jnp.zeros(target.shape, jnp.bfloat16)

    def arrived(copies):
        for copy, sends, receives, target in copies:
            pl.when(receives)(copy.wait_recv)

    for copy in fetches[1:]:
        copy.wait()

    def smooth(zb):
        first, own = (zb * ZB + 1) * rows, (zb * ZB + 2) * rows
        zs = slice(zb * ZB, (zb + 1) * ZB)
        for j in range(blocks):
            near = jnp.concatenate(
                [field[first : first + m + 2 * rows, cols(j)], hlo[1, zs, cols(j)], hhi[0, zs, cols(j)]],
                axis=0,
            )
            value = dot(a_m[...], near) + dot(field[own : own + m, win(j)], sy_m[kind[j]])
            rounded = (0.1 * value).astype(jnp.bfloat16)
            sm[first : first + m, cols(j)] = rounded
            sf[first : first + m, cols(j)] = rounded.astype(jnp.float32)

    for zb in range(groups):
        if zb == 0:
            arrived(z_copies)
        arrived(x_copies[2 * zb : 2 * zb + 2])
        smooth(zb)
    arrived(c_copies)

    one = lambda flag: jnp.where(flag, 1.0, 0.0)
    for j in range(blocks):
        edge_in = jnp.concatenate(
            [field[0 : 3 * rows, cols(j)], field[(planes + 1) * rows :, cols(j)], corners[:, cols(j)]],
            axis=0,
        )
        edge_own = jnp.concatenate(
            [field[rows : 2 * rows, win(j)], field[(planes + 2) * rows : (planes + 3) * rows, win(j)]],
            axis=0,
        )
        edge = 0.1 * (dot(ae_m[...], edge_in) + dot(edge_own, sy_m[kind[j]]))
        sf[0:rows, cols(j)] = (edge[:rows] * one(nearer)).astype(jnp.bfloat16).astype(jnp.float32)
        sf[(planes + 1) * rows :, cols(j)] = (
            (edge[rows:] * one(farther)).astype(jnp.bfloat16).astype(jnp.float32)
        )
        for s, (halo, near, far, own, dst, there) in enumerate(
            ((hlo, 1, 0, 0, slo, lower), (hhi, 0, 1, 3, shi, upper))
        ):
            side_in = jnp.concatenate(
                [halo[near, :, cols(j)], corners[:, cols(j)], halo[far, :, cols(j)], packed[own, :, cols(j)]],
                axis=0,
            )
            side = 0.1 * (dot(be_m[s], side_in) + dot(halo[near, :, win(j)], sy_m[kind[j]]))
            dst[:, cols(j)] = (side * one(there)).astype(jnp.bfloat16)

    def slopes(zb, carry):
        own = pl.multiple_of((zb * ZB + 1) * rows, rows)
        put = pl.multiple_of(zb * ZB * rows, rows)
        zs = pl.ds(pl.multiple_of(zb * ZB, ZB), ZB)
        for j in range(blocks):
            near = jnp.concatenate(
                [sm[pl.ds(own, m), cols(j)], slo[zs, cols(j)], shi[zs, cols(j)]], axis=0
            )
            gx[pl.ds(put, m), cols(j)] = dot(dx_m[...], near)
            gy[pl.ds(put, m), cols(j)] = dot(sm[pl.ds(own, m), win(j)], dy_m[kind[j]])
        return carry

    lax.fori_loop(0, groups, slopes, 0)

    part = width // depths
    halves = rows // 8
    lanes = part // 128
    step = 4

    def owner(i, carry):
        whose = lax.rem(d + 1 + i, depths)

        def piece(p, carry):
            row = pl.multiple_of(lax.rem(p, halves) * 8, 8)
            place = pl.multiple_of((p // halves) * 128, 128)
            col = pl.ds(pl.multiple_of(whose * part + place, 128), 128)

            def spot(z):
                return pl.ds(pl.multiple_of(z * rows + row, 8), 8)

            def march(i, state):
                prev, here, tau, through, total, line, *bends = state
                for u in range(step):
                    z = i * step + u
                    after = sf[spot(z + 2), col]
                    sx, sy = gx[spot(z), col], gy[spot(z), col]
                    sz = after - prev
                    facing = jnp.abs(0.42 * sz + 0.56 * sx)
                    shading = 0.3 + facing * lax.rsqrt(sz * sz + sx * sx + (sy * sy + 0.4))
                    x = jnp.minimum(jnp.maximum(here, tab[0]), tab[count - 1])
                    tops = [jnp.maximum(x, tab[k]) for k in range(1, count - 1)]
                    terms = [tab[5 * count - 1] + tab[4 * count] * x]
                    terms += [tab[4 * count + k] * tops[k - 1] for k in range(1, count - 1)]
                    while len(terms) > 1:
                        terms = [
                            terms[q] + terms[q + 1] if q + 1 < len(terms) else terms[q]
                            for q in range(0, len(terms), 2)
                        ]
                    tau = tau + terms[0]
                    left = jnp.exp2(tau)
                    weight = shading * (through - left)
                    through = left
                    total = total + weight
                    line = line + weight * x
                    bends = [bends[k] + weight * tops[k] for k in range(count - 2)]
                    prev, here = here, after
                return (prev, here, tau, through, total, line, *bends)

            zero = jnp.zeros((8, 128), jnp.float32)
            state = (sf[spot(0), col], sf[spot(1), col], zero, zero + 1.0) + (zero,) * count
            _, _, tau, _, total, line, *bends = lax.fori_loop(0, planes // step, march, state)
            for c in range(3):
                value = tab[count * (c + 2) - 1] * total + tab[count * (c + 1)] * line
                for k in range(1, count - 1):
                    value = value + tab[count * (c + 1) + k] * bends[k - 1]
                stage[whose, c, pl.ds(row, 8), pl.ds(place, 128)] = value
            stage[whose, 3, pl.ds(row, 8), pl.ds(place, 128)] = tau
            return carry

        lax.fori_loop(0, halves * lanes, piece, 0)

        @pl.when(i < depths - 1)
        def _():
            remote(stage.at[whose], parts.at[d], f_send.at[i], f_recv.at[i], whose, t).start()

        return carry

    lax.fori_loop(0, depths, owner, 0)
    parts[d] = stage[d]
    for i in range(depths - 1):
        whose = lax.rem(d + 1 + i, depths)
        source = lax.rem(d - 1 - i + depths, depths)
        remote(stage.at[whose], parts.at[source], f_send.at[i], f_recv.at[i], whose, t).wait_recv()

    for row in range(0, rows, 8):
        for place in range(0, part, 128):
            spots = (slice(row, row + 8), slice(place, place + 128))
            ahead = parts[(0, 3) + spots]
            colors = [parts[(0, c) + spots] for c in range(3)]
            for i in range(1, depths):
                left = jnp.exp2(ahead)
                colors = [colors[c] + left * parts[(i, c) + spots] for c in range(3)]
                ahead = ahead + parts[(i, 3) + spots]
            for c in range(3):
                out[(c,) + spots] = colors[c]
            out[(3,) + spots] = 1.0 - jnp.exp2(ahead)

    for copy, sends, receives, target in z_copies + x_copies + c_copies:
        pl.when(sends)(copy.wait_send)
    for i in range(depths - 1):
        whose = lax.rem(d + 1 + i, depths)
        remote(stage.at[whose], parts.at[d], f_send.at[i], f_recv.at[i], whose, t).wait_send()


def solution(mesh):
    sizes = (mesh.shape["depth"], mesh.shape["tile"])

    def body(volume, knot_pos, knot_color):
        planes, rows, width = volume.shape
        consts = [jnp.asarray(c) for c in constants(planes, rows, width)]
        part = width // sizes[0]
        bf, f32 = jnp.bfloat16, jnp.float32
        dma = pltpu.SemaphoreType.DMA
        smem = pl.BlockSpec(memory_space=pltpu.SMEM)
        anywhere = pl.BlockSpec(memory_space=pl.ANY)
        return pl.pallas_call(
            functools.partial(compute, sizes),
            out_shape=jax.ShapeDtypeStruct((4, rows, part), f32),
            in_specs=[smem, smem] + [anywhere] * (1 + len(consts)),
            out_specs=pl.BlockSpec(memory_space=pltpu.VMEM),
            scratch_shapes=[
                pltpu.VMEM(((planes + 4) * rows, width), bf),
                pltpu.VMEM((4, planes, width), bf),
                pltpu.VMEM((2, planes, width), bf),
                pltpu.VMEM((2, planes, width), bf),
                pltpu.VMEM((4 * ZB, width), bf),
                pltpu.VMEM(((planes + 2) * rows, width), bf),
                pltpu.VMEM((planes, width), bf),
                pltpu.VMEM((planes, width), bf),
                pltpu.VMEM(((planes + 2) * rows, width), f32),
                pltpu.VMEM((planes * rows, width), f32),
                pltpu.VMEM((planes * rows, width), f32),
                pltpu.VMEM((5 * knot_pos.shape[0], 8, 128), f32),
                pltpu.VMEM((sizes[0], 4, rows, part), f32),
                pltpu.VMEM((sizes[0], 4, rows, part), f32),
            ]
            + [pltpu.VMEM(c.shape, c.dtype) for c in consts]
            + [
                dma((planes // ZB,)), dma((len(consts),)),
                dma((2,)), dma((2,)),
                dma((2 * planes // ZB,)), dma((2 * planes // ZB,)),
                dma((4,)), dma((4,)),
                dma((sizes[0] - 1,)), dma((sizes[0] - 1,)),
            ],
            compiler_params=pltpu.CompilerParams(
                vmem_limit_bytes=48 << 20, collective_id=0, has_side_effects=True
            ),
        )(knot_pos, knot_color, volume.reshape(planes * rows, width), *consts)

    in_specs = (P("depth", "tile", None), P(), P())
    return jax.shard_map(
        body, mesh=mesh, in_specs=in_specs, out_specs=P(None, "tile", "depth"), check_vma=False
    )
```

time: 78.5 us -> 50.7 us (0.65)
  the two profiles are of different devices: /device:TPU:8 before, /device:TPU:9 now
where the time goes in v2:
time: 50.7 us; the launch traced here: 50.2 us
  Pallas kernels  40.2 us (79%)
  local copies, waits for them, and re-layouts  9.99 us (20%)
    pallas_call x1, Pallas kernels, body(): pl.pallas_call(functools.partial(compute, sizes), out_shape=jax.ShapeDtyp...  40.2 us
    unnamed x21, local copies, waits for them, and re-layouts  9.99 us

profile of v2, /device:TPU:9, one launch (start us, length us, event | category | flops | bytes accessed | tf_op | source)
XLA Modules:
  0.0 50.2 jit_solution(9609126506188291766)
XLA Ops:
  0.0 0.0 copy-start
  0.0 1.6 %copy-done = bf16[64,16,1024]{2,1,0:T(8,128)(2,1)S(1)} copy-done((bf16[64,16,1024]{2,1,0:T(8,128)(2,1)S(1)}, bf16[64,16,1024]{2,1,0:T(8,128)(2,1)}, u32[]{:S(2)}) %copy-start) | copy-done | bytes 2097176
  1.6 0.0 copy-start.1
  1.6 1.1 %copy-done.1 = bf16[3,512,256]{2,1,0:T(8,128)(2,1)S(1)} copy-done((bf16[3,512,256]{2,1,0:T(8,128)(2,1)S(1)}, bf16[3,512,256]{2,1,0:T(8,128)(2,1)}, u32[]{:S(2)}) %copy-start.1) | copy-done | bytes 786456
  2.7 0.0 copy-start.2
  2.7 1.1 %copy-done.2 = bf16[3,512,256]{2,1,0:T(8,128)(2,1)S(1)} copy-done((bf16[3,512,256]{2,1,0:T(8,128)(2,1)S(1)}, bf16[3,512,256]{2,1,0:T(8,128)(2,1)}, u32[]{:S(2)}) %copy-start.2) | copy-done | bytes 786456
  3.9 0.0 copy-start.3
  3.9 0.9 %copy-done.3 = bf16[256,288]{1,0:T(8,128)(2,1)S(1)} copy-done((bf16[256,288]{1,0:T(8,128)(2,1)S(1)}, bf16[256,288]{1,0:T(8,128)(2,1)}, u32[]{:S(2)}) %copy-start.3) | copy-done | bytes 147480
  4.8 0.0 copy-start.4
  4.8 0.9 %copy-done.4 = bf16[256,320]{1,0:T(8,128)(2,1)S(1)} copy-done((bf16[256,320]{1,0:T(8,128)(2,1)S(1)}, bf16[256,320]{1,0:T(8,128)(2,1)}, u32[]{:S(2)}) %copy-start.4) | copy-done | bytes 163864
  5.7 0.0 copy-start.5
  5.7 0.8 %copy-done.5 = bf16[2,64,256]{2,1,0:T(8,128)(2,1)S(1)} copy-done((bf16[2,64,256]{2,1,0:T(8,128)(2,1)S(1)}, bf16[2,64,256]{2,1,0:T(8,128)(2,1)}, u32[]{:S(2)}) %copy-start.5) | copy-done | bytes 65560
  6.6 0.0 copy-start.6
  6.6 0.8 %copy-done.6 = bf16[64,256]{1,0:T(8,128)(2,1)S(1)} copy-done((bf16[64,256]{1,0:T(8,128)(2,1)S(1)}, bf16[64,256]{1,0:T(8,128)(2,1)}, u32[]{:S(2)}) %copy-start.6) | copy-done | bytes 32792
  7.3 0.0 copy-start.7
  7.3 0.7 %copy-done.7 = bf16[32,160]{1,0:T(8,128)(2,1)S(1)} copy-done((bf16[32,160]{1,0:T(8,128)(2,1)S(1)}, bf16[32,160]{1,0:T(8,128)(2,1)}, u32[]{:S(2)}) %copy-start.7) | copy-done | bytes 10264
  8.0 0.0 copy-start.8
  8.0 0.7 %copy-done.8 = s32[4,16]{1,0:T(4,128)S(1)} copy-done((s32[4,16]{1,0:T(4,128)S(1)}, s32[4,16]{1,0:T(4,128)}, u32[]{:S(2)}) %copy-start.8) | copy-done | bytes 280
  8.7 0.0 copy-start.9
  8.7 0.7 %copy-done.9 = s32[16]{0:T(128)S(1)} copy-done((s32[16]{0:T(128)S(1)}, s32[16]{0:T(128)}, u32[]{:S(2)}) %copy-start.9) | copy-done | bytes 88
  9.4 40.2 %shard_map.100 = f32[4,16,256]{2,1,0:T(8,128)S(1)} custom-call(s32[16]{0:T(128)S(1)} %copy-done.9, s32[4,16]{1,0:T(4,128)S(1)} %copy-done.8, bf16[1024,1024]{1,0:T(8,128)(2,1)S(1)} %bitcast.1, bf16[64,256]{1,0:T(8,128)(2,1)S(1)} %copy-done.6, bf16[3,512,256]{2,1,0:T(8,128)(2,1)S(1)} %copy-done.2, bf16[256,320]{1,0:T(8,128)(2,1)S(1)} %copy-done.4, ...), custom_call_target="tpu_custom_call" | custom-call | tf_op jit(solution)/shard_map/pallas_call | solution.py:422
  49.6 0.6 %copy.12 = f32[4,16,256]{2,1,0:T(8,128)} copy(f32[4,16,256]{2,1,0:T(8,128)S(1)} %shard_map.100) | data formatting | bytes 131072
Async XLA Ops:
  0.0 1.6 %copy-start = (bf16[64,16,1024]{2,1,0:T(8,128)(2,1)S(1)}, bf16[64,16,1024]{2,1,0:T(8,128)(2,1)}, u32[]{:S(2)}) copy-start(bf16[64,16,1024]{2,1,0:T(8,128)(2,1)} %param.10) | copy-start | bytes 6291460
  1.6 1.1 %copy-start.1 = (bf16[3,512,256]{2,1,0:T(8,128)(2,1)S(1)}, bf16[3,512,256]{2,1,0:T(8,128)(2,1)}, u32[]{:S(2)}) copy-start(bf16[3,512,256]{2,1,0:T(8,128)(2,1)} %constant.20.clone.dy_h) | copy-start | bytes 2359300
  2.7 1.1 %copy-start.2 = (bf16[3,512,256]{2,1,0:T(8,128)(2,1)S(1)}, bf16[3,512,256]{2,1,0:T(8,128)(2,1)}, u32[]{:S(2)}) copy-start(bf16[3,512,256]{2,1,0:T(8,128)(2,1)} %constant.15.clone.sy_h) | copy-start | bytes 2359300
  3.9 0.9 %copy-start.3 = (bf16[256,288]{1,0:T(8,128)(2,1)S(1)}, bf16[256,288]{1,0:T(8,128)(2,1)}, u32[]{:S(2)}) copy-start(bf16[256,288]{1,0:T(8,128)(2,1)} %constant.19.clone.dx_h) | copy-start | bytes 442372
  4.8 0.9 %copy-start.4 = (bf16[256,320]{1,0:T(8,128)(2,1)S(1)}, bf16[256,320]{1,0:T(8,128)(2,1)}, u32[]{:S(2)}) copy-start(bf16[256,320]{1,0:T(8,128)(2,1)} %constant.16.clone.a_h) | copy-start | bytes 491524
  5.7 0.8 %copy-start.5 = (bf16[2,64,256]{2,1,0:T(8,128)(2,1)S(1)}, bf16[2,64,256]{2,1,0:T(8,128)(2,1)}, u32[]{:S(2)}) copy-start(bf16[2,64,256]{2,1,0:T(8,128)(2,1)} %constant.18.clone.be_h) | copy-start | bytes 196612
  6.6 0.8 %copy-start.6 = (bf16[64,256]{1,0:T(8,128)(2,1)S(1)}, bf16[64,256]{1,0:T(8,128)(2,1)}, u32[]{:S(2)}) copy-start(bf16[64,256]{1,0:T(8,128)(2,1)} %constant.14.clone.pack_h) | copy-start | bytes 98308
  7.3 0.7 %copy-start.7 = (bf16[32,160]{1,0:T(8,128)(2,1)S(1)}, bf16[32,160]{1,0:T(8,128)(2,1)}, u32[]{:S(2)}) copy-start(bf16[32,160]{1,0:T(8,128)(2,1)} %constant.17.clone.ae_h) | copy-start | bytes 30724
  8.0 0.7 %copy-start.8 = (s32[4,16]{1,0:T(4,128)S(1)}, s32[4,16]{1,0:T(4,128)}, u32[]{:S(2)}) copy-start(s32[4,16]{1,0:T(4,128)} %knot_color.1) | copy-start | bytes 772
  8.7 0.7 %copy-start.9 = (s32[16]{0:T(128)S(1)}, s32[16]{0:T(128)}, u32[]{:S(2)}) copy-start(s32[16]{0:T(128)} %knot_pos.1) | copy-start | bytes 196

commit v3 on v2

--- a/solution.py
+++ b/solution.py
@@ -56,26 +56,23 @@
             a[o, c + 1 if x < rows - 1 else m + 2 * rows + ZB + z] += 1
             dx[o, o - 1 if x else m + z] -= 1
             dx[o, o + 1 if x < rows - 1 else m + ZB + z] += 1
-    ae = np.zeros((2 * rows, 6 * rows + 4 * ZB), np.float32)
-    low_corner = [ZB - 1, 2 * ZB]
-    high_corner = [2 * ZB - 1, 3 * ZB]
+    ae = np.zeros((2, rows, 3 * rows + 2 * ZB), np.float32)
     for e in range(2):
+        beside = 0 if e else ZB - 1
         for x in range(rows):
-            o = e * rows + x
-            c = 3 * rows * e + rows + x
-            ae[o, c] += 4
-            ae[o, c - rows] += 1
-            ae[o, c + rows] += 1
-            ae[o, c - 1 if x else 6 * rows + low_corner[e]] += 1
-            ae[o, c + 1 if x < rows - 1 else 6 * rows + high_corner[e]] += 1
-    be = np.zeros((2, planes, 3 * planes + 4 * ZB), np.float32)
-    for s, corner in enumerate((low_corner, high_corner)):
-        for z in range(planes):
-            be[s, z, z] += 4
-            be[s, z, z - 1 if z else planes + corner[0]] += 1
-            be[s, z, z + 1 if z < planes - 1 else planes + corner[1]] += 1
-            be[s, z, planes + 4 * ZB + z] += 1
-            be[s, z, 2 * planes + 4 * ZB + z] += 1
+            c = rows + x
+            ae[e, x, c] += 4
+            ae[e, x, c - rows] += 1
+            ae[e, x, c + rows] += 1
+            ae[e, x, c - 1 if x else 3 * rows + beside] += 1
+            ae[e, x, c + 1 if x < rows - 1 else 3 * rows + ZB + beside] += 1
+    be = np.zeros((ZB, 5 * ZB), np.float32)
+    for z in range(ZB):
+        be[z, ZB + z] += 4
+        be[z, ZB + z - 1] += 1
+        be[z, ZB + z + 1] += 1
+        be[z, 3 * ZB + z] += 1
+        be[z, 4 * ZB + z] += 1
     pack = np.zeros((4 * ZB, m), np.float32)
     for r, row in enumerate((0, 1, rows - 2, rows - 1)):
         for z in range(ZB):
@@ -91,7 +88,7 @@
 def compute(
     sizes, knot_pos, knot_color, vol,
     pack_h, sy_h, a_h, ae_h, be_h, dx_h, dy_h,
-    out, field, packed, hlo, hhi, corners, sm, slo, shi, sf, gx, gy, tab, stage, parts,
+    out, field, packed, hlo, hhi, corners, sm, slo, shi, sf, gx, gy, tab, stage, parts, sums,
     pack_m, sy_m, a_m, ae_m, be_m, dx_m, dy_m,
     vol_sem, const_sem, z_send, z_recv, x_send, x_recv, c_send, c_recv, f_send, f_recv,
 ):
@@ -243,7 +240,7 @@
                 sends, receives, target,
             )
         )
-    for copy, sends, receives, target in z_copies + x_copies + c_copies:
+    for copy, sends, receives, target in z_copies + x_copies[:2] + c_copies + x_copies[2:]:
         pl.when(sends)(copy.start)
 
     for copy, sends, receives, target in z_copies + x_copies + c_copies:
@@ -272,99 +269,115 @@
             sm[first : first + m, cols(j)] = rounded
             sf[first : first + m, cols(j)] = rounded.astype(jnp.float32)
 
-    for zb in range(groups):
-        if zb == 0:
-            arrived(z_copies)
-        arrived(x_copies[2 * zb : 2 * zb + 2])
-        smooth(zb)
-    arrived(c_copies)
-
     one = lambda flag: jnp.where(flag, 1.0, 0.0)
-    for j in range(blocks):
-        edge_in = jnp.concatenate(
-            [field[0 : 3 * rows, cols(j)], field[(planes + 1) * rows :, cols(j)], corners[:, cols(j)]],
-            axis=0,
-        )
-        edge_own = jnp.concatenate(
-            [field[rows : 2 * rows, win(j)], field[(planes + 2) * rows : (planes + 3) * rows, win(j)]],
-            axis=0,
-        )
-        edge = 0.1 * (dot(ae_m[...], edge_in) + dot(edge_own, sy_m[kind[j]]))
-        sf[0:rows, cols(j)] = (edge[:rows] * one(nearer)).astype(jnp.bfloat16).astype(jnp.float32)
-        sf[(planes + 1) * rows :, cols(j)] = (
-            (edge[rows:] * one(farther)).astype(jnp.bfloat16).astype(jnp.float32)
-        )
-        for s, (halo, near, far, own, dst, there) in enumerate(
-            ((hlo, 1, 0, 0, slo, lower), (hhi, 0, 1, 3, shi, upper))
-        ):
-            side_in = jnp.concatenate(
-                [halo[near, :, cols(j)], corners[:, cols(j)], halo[far, :, cols(j)], packed[own, :, cols(j)]],
-                axis=0,
-            )
-            side = 0.1 * (dot(be_m[s], side_in) + dot(halo[near, :, win(j)], sy_m[kind[j]]))
-            dst[:, cols(j)] = (side * one(there)).astype(jnp.bfloat16)
-
-    def slopes(zb, carry):
-        own = pl.multiple_of((zb * ZB + 1) * rows, rows)
-        put = pl.multiple_of(zb * ZB * rows, rows)
-        zs = pl.ds(pl.multiple_of(zb * ZB, ZB), ZB)
+
+    def edge(first, put, corner, there):
         for j in range(blocks):
             near = jnp.concatenate(
-                [sm[pl.ds(own, m), cols(j)], slo[zs, cols(j)], shi[zs, cols(j)]], axis=0
-            )
-            gx[pl.ds(put, m), cols(j)] = dot(dx_m[...], near)
-            gy[pl.ds(put, m), cols(j)] = dot(sm[pl.ds(own, m), win(j)], dy_m[kind[j]])
-        return carry
-
-    lax.fori_loop(0, groups, slopes, 0)
+                [field[first : first + 3 * rows, cols(j)], corners[corner : corner + 2 * ZB, cols(j)]],
+                axis=0,
+            )
+            own = field[first + rows : first + 2 * rows, win(j)]
+            value = 0.1 * (dot(ae_m[corner // (2 * ZB)], near) + dot(own, sy_m[kind[j]]))
+            value = (value * one(there)).astype(jnp.bfloat16)
+            sf[put : put + rows, cols(j)] = value.astype(jnp.float32)
+
+    def sides(zb):
+        zs = slice(zb * ZB, (zb + 1) * ZB)
+        for j in range(blocks):
+            for s, (halo, near, far, own, dst, there) in enumerate(
+                ((hlo, 1, 0, 0, slo, lower), (hhi, 0, 1, 3, shi, upper))
+            ):
+
+                def block(b):
+                    if b < 0:
+                        return corners[s * ZB : (s + 1) * ZB, cols(j)]
+                    if b == groups:
+                        return corners[(2 + s) * ZB : (3 + s) * ZB, cols(j)]
+                    return halo[near, b * ZB : (b + 1) * ZB, cols(j)]
+
+                side_in = jnp.concatenate(
+                    [block(zb - 1), block(zb), block(zb + 1), halo[far, zs, cols(j)], packed[own, zs, cols(j)]],
+                    axis=0,
+                )
+                side = 0.1 * (dot(be_m[...], side_in) + dot(halo[near, zs, win(j)], sy_m[kind[j]]))
+                dst[:, cols(j)] = (side * one(there)).astype(jnp.bfloat16)
+
+    def slopes(zb):
+        own = (zb * ZB + 1) * rows
+        for j in range(blocks):
+            near = jnp.concatenate(
+                [sm[own : own + m, cols(j)], slo[:, cols(j)], shi[:, cols(j)]], axis=0
+            )
+            gx[:, cols(j)] = dot(dx_m[...], near)
+            gy[:, cols(j)] = dot(sm[own : own + m, win(j)], dy_m[kind[j]])
 
     part = width // depths
     halves = rows // 8
     lanes = part // 128
     step = 4
-
-    def owner(i, carry):
+    zero = jnp.zeros((8, 128), jnp.float32)
+
+    def composite(zb, row, col, n):
+        def spot(z):
+            return pl.ds(pl.multiple_of(z * rows + row, 8), 8)
+
+        def march(i, state):
+            prev, here, tau, through, total, line, *bends = state
+            for u in range(step):
+                z = i * step + u
+                after = sf[spot(zb * ZB + z + 2), col]
+                sx, sy = gx[spot(z), col], gy[spot(z), col]
+                sz = after - prev
+                facing = jnp.abs(0.42 * sz + 0.56 * sx)
+                shading = 0.3 + facing * lax.rsqrt(sz * sz + sx * sx + (sy * sy + 0.4))
+                x = jnp.minimum(jnp.maximum(here, tab[0]), tab[count - 1])
+                tops = [jnp.maximum(x, tab[k]) for k in range(1, count - 1)]
+                terms = [tab[5 * count - 1] + tab[4 * count] * x]
+                terms += [tab[4 * count + k] * tops[k - 1] for k in range(1, count - 1)]
+                while len(terms) > 1:
+                    terms = [
+                        terms[q] + terms[q + 1] if q + 1 < len(terms) else terms[q]
+                        for q in range(0, len(terms), 2)
+                    ]
+                tau = tau + terms[0]
+                left = jnp.exp2(tau)
+                weight = shading * (through - left)
+                through = left
+                total = total + weight
+                line = line + weight * x
+                bends = [bends[k] + weight * tops[k] for k in range(count - 2)]
+                prev, here = here, after
+            return (prev, here, tau, through, total, line, *bends)
+
+        state = (sf[spot(zb * ZB), col], sf[spot(zb * ZB + 1), col])
+        if zb == 0:
+            state += (zero, zero + 1.0) + (zero,) * count
+        else:
+            state += tuple(sums[n, k] for k in range(count + 2))
+        return lax.fori_loop(0, ZB // step, march, state)[2:]
+
+    def middle(zb):
+        def piece(p, carry):
+            row = pl.multiple_of(lax.rem(p, halves) * 8, 8)
+            col = pl.ds(pl.multiple_of((p // halves) * 128, 128), 128)
+            state = composite(zb, row, col, p)
+            for k in range(count + 2):
+                sums[p, k] = state[k]
+            return carry
+
+        lax.fori_loop(0, halves * (width // 128), piece, 0)
+
+    def finish(i, carry):
         whose = lax.rem(d + 1 + i, depths)
 
         def piece(p, carry):
             row = pl.multiple_of(lax.rem(p, halves) * 8, 8)
             place = pl.multiple_of((p // halves) * 128, 128)
             col = pl.ds(pl.multiple_of(whose * part + place, 128), 128)
-
-            def spot(z):
-                return pl.ds(pl.multiple_of(z * rows + row, 8), 8)
-
-            def march(i, state):
-                prev, here, tau, through, total, line, *bends = state
-                for u in range(step):
-                    z = i * step + u
-                    after = sf[spot(z + 2), col]
-                    sx, sy = gx[spot(z), col], gy[spot(z), col]
-                    sz = after - prev
-                    facing = jnp.abs(0.42 * sz + 0.56 * sx)
-                    shading = 0.3 + facing * lax.rsqrt(sz * sz + sx * sx + (sy * sy + 0.4))
-                    x = jnp.minimum(jnp.maximum(here, tab[0]), tab[count - 1])
-                    tops = [jnp.maximum(x, tab[k]) for k in range(1, count - 1)]
-                    terms = [tab[5 * count - 1] + tab[4 * count] * x]
-                    terms += [tab[4 * count + k] * tops[k - 1] for k in range(1, count - 1)]
-                    while len(terms) > 1:
-                        terms = [
-                            terms[q] + terms[q + 1] if q + 1 < len(terms) else terms[q]
-                            for q in range(0, len(terms), 2)
-                        ]
-                    tau = tau + terms[0]
-                    left = jnp.exp2(tau)
-                    weight = shading * (through - left)
-                    through = left
-                    total = total + weight
-                    line = line + weight * x
-                    bends = [bends[k] + weight * tops[k] for k in range(count - 2)]
-                    prev, here = here, after
-                return (prev, here, tau, through, total, line, *bends)
-
-            zero = jnp.zeros((8, 128), jnp.float32)
-            state = (sf[spot(0), col], sf[spot(1), col], zero, zero + 1.0) + (zero,) * count
-            _, _, tau, _, total, line, *bends = lax.fori_loop(0, planes // step, march, state)
+            tau, _, total, line, *bends = composite(
+                groups - 1, row, col, whose * halves * lanes + p
+            )
             for c in range(3):
                 value = tab[count * (c + 2) - 1] * total + tab[count * (c + 1)] * line
                 for k in range(1, count - 1):
@@ -381,7 +394,24 @@
 
         return carry
 
-    lax.fori_loop(0, depths, owner, 0)
+    arrived(z_copies)
+    arrived(x_copies[:2])
+    smooth(0)
+    arrived(c_copies)
+    edge(0, 0, 0, nearer)
+    for zb in range(groups):
+        if zb < groups - 1:
+            arrived(x_copies[2 * zb + 2 : 2 * zb + 4])
+            smooth(zb + 1)
+        else:
+            edge((planes + 1) * rows, (planes + 1) * rows, 2 * ZB, farther)
+        sides(zb)
+        slopes(zb)
+        if zb < groups - 1:
+            middle(zb)
+        else:
+            lax.fori_loop(0, depths, finish, 0)
+
     parts[d] = stage[d]
     for i in range(depths - 1):
         whose = lax.rem(d + 1 + i, depths)
@@ -418,7 +448,7 @@
         bf, f32 = jnp.bfloat16, jnp.float32
         dma = pltpu.SemaphoreType.DMA
         smem = pl.BlockSpec(memory_space=pltpu.SMEM)
-        anywhere = pl.BlockSpec(memory_space=pl.ANY)
+        anywhere = pl.BlockSpec(memory_space=pltpu.HBM)
         return pl.pallas_call(
             functools.partial(compute, sizes),
             out_shape=jax.ShapeDtypeStruct((4, rows, part), f32),
@@ -431,14 +461,15 @@
                 pltpu.VMEM((2, planes, width), bf),
                 pltpu.VMEM((4 * ZB, width), bf),
                 pltpu.VMEM(((planes + 2) * rows, width), bf),
-                pltpu.VMEM((planes, width), bf),
-                pltpu.VMEM((planes, width), bf),
+                pltpu.VMEM((ZB, width), bf),
+                pltpu.VMEM((ZB, width), bf),
                 pltpu.VMEM(((planes + 2) * rows, width), f32),
-                pltpu.VMEM((planes * rows, width), f32),
-                pltpu.VMEM((planes * rows, width), f32),
+                pltpu.VMEM((ZB * rows, width), f32),
+                pltpu.VMEM((ZB * rows, width), f32),
                 pltpu.VMEM((5 * knot_pos.shape[0], 8, 128), f32),
                 pltpu.VMEM((sizes[0], 4, rows, part), f32),
                 pltpu.VMEM((sizes[0], 4, rows, part), f32),
+                pltpu.VMEM((rows // 8 * (width // 128), knot_pos.shape[0] + 2, 8, 128), f32),
             ]
             + [pltpu.VMEM(c.shape, c.dtype) for c in consts]
             + [
@@ -449,7 +480,7 @@
                 dma((sizes[0] - 1,)), dma((sizes[0] - 1,)),
             ],
             compiler_params=pltpu.CompilerParams(
-                vmem_limit_bytes=48 << 20, collective_id=0, has_side_effects=True
+                vmem_limit_bytes=62 << 20, collective_id=0, has_side_effects=True
             ),
         )(knot_pos, knot_color, volume.reshape(planes * rows, width), *consts)
 

time: 50.7 us -> 43.8 us (0.86)
  the two profiles are of different devices: /device:TPU:9 before, /device:TPU:21 now
where the time goes in v3:
time: 43.8 us; the launch traced here: 43.4 us
  Pallas kernels  41.9 us (96%)
  local copies, waits for them, and re-layouts  1.47 us (3%)
    pallas_call x1, Pallas kernels, body(): pl.pallas_call(functools.partial(compute, sizes), out_shape=jax.ShapeDtyp...  41.9 us
    unnamed x1, local copies, waits for them, and re-layouts  1.47 us

profile of v3, /device:TPU:21, one launch (start us, length us, event | category | flops | bytes accessed | tf_op | source)
XLA Modules:
  0.0 43.4 jit_solution(8118798513805484197)
XLA Ops:
  0.0 41.9 %shard_map.100 = f32[4,16,256]{2,1,0:T(8,128)} custom-call(s32[16]{0:T(128)} %knot_pos.1, s32[4,16]{1,0:T(4,128)} %knot_color.1, bf16[1024,1024]{1,0:T(8,128)(2,1)} %bitcast.1, bf16[64,256]{1,0:T(8,128)(2,1)} %constant.14.clone.pack_h, bf16[3,512,256]{2,1,0:T(8,128)(2,1)} %constant.15.clone.sy_h, bf16[256,320]{1,0:T(8,128)(2,1)} %constant.16.clone.a_h, ...), custom_call_target="tpu_custom_call" | custom-call | tf_op jit(solution)/shard_map/pallas_call | solution.py:452
  41.9 1.5 %copy.12 = f32[4,16,256]{2,1,0:T(8,128)} copy(f32[4,16,256]{2,1,0:T(8,128)} %shard_map.100) | data formatting | bytes 131072

commit v4 on v3

--- a/solution.py
+++ b/solution.py
@@ -240,8 +240,11 @@
                 sends, receives, target,
             )
         )
-    for copy, sends, receives, target in z_copies + x_copies[:2] + c_copies + x_copies[2:]:
-        pl.when(sends)(copy.start)
+    def depart(copies):
+        for copy, sends, receives, target in copies:
+            pl.when(sends)(copy.start)
+
+    depart(x_copies[:2] + z_copies + c_copies[:2] + x_copies[2:4])
 
     for copy, sends, receives, target in z_copies + x_copies + c_copies:
 
@@ -394,16 +397,21 @@
 
         return carry
 
-    arrived(z_copies)
+    arrived(z_copies[:1])
     arrived(x_copies[:2])
     smooth(0)
-    arrived(c_copies)
+    arrived(c_copies[:2])
     edge(0, 0, 0, nearer)
     for zb in range(groups):
         if zb < groups - 1:
             arrived(x_copies[2 * zb + 2 : 2 * zb + 4])
+            if zb == 0:
+                depart(x_copies[4:] + c_copies[2:])
+            if zb == groups - 2:
+                arrived(z_copies[1:])
             smooth(zb + 1)
         else:
+            arrived(c_copies[2:])
             edge((planes + 1) * rows, (planes + 1) * rows, 2 * ZB, farther)
         sides(zb)
         slopes(zb)

time: 43.8 us -> 41 us (0.936)
  Pallas kernels: 41.9 us -> 39.3 us
    pallas_call x1, Pallas kernels: 41.9 us -> 39.3 us  [body(): pl.pallas_call(functools.partial(compute, sizes), out_shape=jax.ShapeDtyp...]
where the time goes in v4:
time: 41 us; the launch traced here: 40.8 us
  Pallas kernels  39.3 us (96%)
  local copies, waits for them, and re-layouts  1.47 us (4%)
    pallas_call x1, Pallas kernels, body(): pl.pallas_call(functools.partial(compute, sizes), out_shape=jax.ShapeDtyp...  39.3 us
    unnamed x1, local copies, waits for them, and re-layouts  1.47 us

profile of v4, /device:TPU:21, one launch (start us, length us, event | category | flops | bytes accessed | tf_op | source)
XLA Modules:
  0.0 40.8 jit_solution(11951955617089602073)
XLA Ops:
  0.0 39.3 %shard_map.100 = f32[4,16,256]{2,1,0:T(8,128)} custom-call(s32[16]{0:T(128)} %knot_pos.1, s32[4,16]{1,0:T(4,128)} %knot_color.1, bf16[1024,1024]{1,0:T(8,128)(2,1)} %bitcast.1, bf16[64,256]{1,0:T(8,128)(2,1)} %constant.14.clone.pack_h, bf16[3,512,256]{2,1,0:T(8,128)(2,1)} %constant.15.clone.sy_h, bf16[256,320]{1,0:T(8,128)(2,1)} %constant.16.clone.a_h, ...), custom_call_target="tpu_custom_call" | custom-call | tf_op jit(solution)/shard_map/pallas_call | solution.py:460
  39.3 1.5 %copy.12 = f32[4,16,256]{2,1,0:T(8,128)} copy(f32[4,16,256]{2,1,0:T(8,128)} %shard_map.100) | data formatting | bytes 131072

commit v5 on v4

--- a/solution.py
+++ b/solution.py
@@ -318,7 +318,7 @@
     part = width // depths
     halves = rows // 8
     lanes = part // 128
-    step = 4
+    step = 8
     zero = jnp.zeros((8, 128), jnp.float32)
 
     def composite(zb, row, col, n):

time: 41 us -> 40.4 us (0.985)
  Pallas kernels: 39.3 us -> 38.7 us
    pallas_call x1, Pallas kernels: 39.3 us -> 38.7 us  [body(): pl.pallas_call(functools.partial(compute, sizes), out_shape=jax.ShapeDtyp...]
where the time goes in v5:
time: 40.4 us; the launch traced here: 40.2 us
  Pallas kernels  38.7 us (96%)
  local copies, waits for them, and re-layouts  1.47 us (4%)
    pallas_call x1, Pallas kernels, body(): pl.pallas_call(functools.partial(compute, sizes), out_shape=jax.ShapeDtyp...  38.7 us
    unnamed x1, local copies, waits for them, and re-layouts  1.47 us

profile of v5, /device:TPU:21, one launch (start us, length us, event | category | flops | bytes accessed | tf_op | source)
XLA Modules:
  0.0 40.2 jit_solution(6913899140129869270)
XLA Ops:
  0.0 38.7 %shard_map.100 = f32[4,16,256]{2,1,0:T(8,128)} custom-call(s32[16]{0:T(128)} %knot_pos.1, s32[4,16]{1,0:T(4,128)} %knot_color.1, bf16[1024,1024]{1,0:T(8,128)(2,1)} %bitcast.1, bf16[64,256]{1,0:T(8,128)(2,1)} %constant.14.clone.pack_h, bf16[3,512,256]{2,1,0:T(8,128)(2,1)} %constant.15.clone.sy_h, bf16[256,320]{1,0:T(8,128)(2,1)} %constant.16.clone.a_h, ...), custom_call_target="tpu_custom_call" | custom-call | tf_op jit(solution)/shard_map/pallas_call | solution.py:460
  38.7 1.5 %copy.12 = f32[4,16,256]{2,1,0:T(8,128)} copy(f32[4,16,256]{2,1,0:T(8,128)} %shard_map.100) | data formatting | bytes 131072
